TPU v7x, 32 devices: a whole 2x2x4 slice. The times are simulated.
32 devices in a mesh: brick: 8 (over y, x, core), grp: 4 (over z).
Axes of the slice: x: 2, y: 2, z: 4, core: 2. Of those that a mesh axis runs over, the one named last changes fastest.
Arguments:
- features: bfloat16 [262144, 128], P(('brick', 'grp')), may hold values from -6 to 6
- neighbors: int32 [262144, 27], P(('brick', 'grp')), may hold values from 0 to 12288, as said below
- send_low: int32 [65536], P(('brick', 'grp')), may hold values from 0 to 8191, as said below
- send_high: int32 [65536], P(('brick', 'grp')), may hold values from 0 to 8191, as said below
- send_slot: int32 [393216], P(('brick', 'grp')), may hold values from 0 to 8192, as said below
- recv_slot: int32 [262144], P(('brick', 'grp')), may hold values from 0 to 12287, as said below
- kernel: bfloat16 [27, 128, 128], P(None, None, 'grp'), may hold values from -0.109375 to 0.109375
- norm_gain: float32 [128], replicated, may hold values from 0.5 to 1.5
- norm_shift: float32 [128], replicated, may hold values from -3 to 3
Outputs:
- serial: bfloat16 [262144, 128], P(('brick', 'grp'))
Inputs may be any that keep to these rules, and one draw needn't show every extreme that they name: `neighbors`: an entry below 8192 is a row of the brick itself; 8192 + i is the i-th row sent up by the brick one slab lower; 10240 + i the i-th row sent down by the brick one slab higher; 12288 means no neighbour. Offset k = 9 (dx + 1) + 3 (dy + 1) + (dz + 1); offsets with dx = 0 refer only to the brick's own rows or to no neighbour; offset 13 is the voxel itself; no entry refers to a brick that does not exist. `send_low`: the 2048 entries of a brick are distinct rows of it. `send_high`: the 2048 entries of a brick are distinct rows of it. `send_slot`: 8192 marks an empty slot; every row of a brick is carried by exactly one slot; a brick fills between 512 and 1536 slots for each shard of its scan, the slots t * 1536 + c with c below that count, and every shard receives 8192 rows in all. `recv_slot`: the 8192 entries of a shard are exactly its filled received slots, each once.
All inputs are finite; a program needn't handle non-finite values.
Results may differ from a plain program's by a relative error of at most 0.001.
Values may be sent and summed in bfloat16 or wider, within the bound.
A program may use at most 64 MiB of HBM per device.

v0:
```python
import jax
import jax.numpy as jnp
from jax import lax
from jax.sharding import PartitionSpec as P


def shifted(block, axis, distance):
    devices = range(lax.axis_size(axis))
    route = [(i - distance, i) for i in devices if i - distance in devices]
    return lax.ppermute(block, axis, route)


def convolve(extended, columns, kernel):

    def advance(summed, packed):
        column, weight_mat = packed
        picked = jnp.take(extended, column, axis=0)
        return (summed + jnp.dot(picked, weight_mat, preferred_element_type=jnp.float32), None)

    initial = jnp.zeros((columns.shape[1], kernel.shape[2]), jnp.float32)
    return lax.scan(advance, initial, (columns, kernel))[0]


def body(
    features, neighbors, send_low, send_high, send_slot, recv_slot, kernel, norm_gain, norm_shift
):
    row_count, channels = features.shape
    zero_row = jnp.zeros((1, channels), jnp.bfloat16)
    weights = lax.all_gather(kernel, "grp", axis=2, tiled=True)
    upward = jnp.take(features, send_high, axis=0)
    downward = jnp.take(features, send_low, axis=0)
    from_lower = shifted(upward, "brick", 1)
    from_upper = shifted(downward, "brick", -1)
    columns = neighbors.T
    extended = jnp.concatenate([features, from_lower, from_upper, zero_row], axis=0)
    summed = convolve(extended, columns, weights)
    centered = summed - jnp.mean(summed, axis=-1, keepdims=True)
    spread_sq = jnp.mean(centered * centered, axis=-1, keepdims=True)
    normed = centered * lax.rsqrt(spread_sq + 1e-05) * norm_gain + norm_shift
    blended = (features.astype(jnp.float32) + jax.nn.silu(normed)).astype(jnp.bfloat16)
    slab_count = lax.axis_size("brick")
    capacity = send_slot.shape[0] // slab_count
    padded = jnp.concatenate([blended, zero_row], axis=0)
    outbox = jnp.take(padded, send_slot, axis=0)
    arrived = lax.all_to_all(
        outbox.reshape(slab_count, capacity, channels),
        "brick",
        split_axis=0,
        concat_axis=0,
        tiled=True,
    )
    return jnp.take(arrived.reshape(slab_count * capacity, channels), recv_slot, axis=0)


def solution(mesh):
    return jax.shard_map(
        body,
        mesh=mesh,
        in_specs=(
            P(("brick", "grp"), None),
            P(("brick", "grp"), None),
            P(("brick", "grp")),
            P(("brick", "grp")),
            P(("brick", "grp")),
            P(("brick", "grp")),
            P(None, None, "grp"),
            P(),
            P(),
        ),
        out_specs=P(("brick", "grp"), None),
        check_vma=False,
    )
```

profile of v0, /device:TPU:1, one launch (start us, length us, event | category | flops | bytes accessed | tf_op | source)
XLA Modules:
  0.0 1222.7 jit_solution(5095420404297593655)
XLA Ops:
  22.6 19.7 %all_gather.3 = bf16[27,128,128]{1,2,0:T(8,128)(2,1)} all-gather(bf16[27,128,32]{1,2,0:T(8,128)(2,1)S(1)} %copy-done.3), channel_id=1, replica_groups=mesh['brick'=8,'grp'=4] {'grp'}, dimensions={2}, use_global_device_ids=true | all-gather | bytes 1105920 | tf_op jit(solution)/shard_map/all_gather | solution.py:29
  42.4 10.2 maximum_maximum_fusion
  52.6 1030.0 %while.11 = (s32[]{:T(128)}, f32[8192,128]{1,0:T(8,128)}, s32[27,8192]{1,0:T(8,128)}, bf16[12289,128]{1,0:T(8,128)(2,1)S(1)}, bf16[27,128,128]{1,2,0:T(8,128)(2,1)}, /*index=5*/s32[]{:T(128)}, s32[]{:T(128)}) while((s32[]{:T(128)}, f32[8192,128]{1,0:T(8,128)}, s32[27,8192]{1,0:T(8,128)}, bf16[12289,128]{1,0:T(8,128)(2,1)S(1)}, ...), condition=%wide.region_1.3_spmd.clone, body=%wide.region_0.0_spmd.clone.sunk | while | flops 271663104 | bytes 14959195 | solution.py:21
  53.6 29.5 %gather_fusion = bf16[8192,128]{1,0:T(8,128)(2,1)} fusion(bf16[12289,128]{1,0:T(8,128)(2,1)S(1)} %get-tuple-element.121, s32[8192]{0:T(1024)S(1)} %broadcast_clamp_fusion.2), kind=kCustom, calls=%fused_computation.1.clone.clone.1 | custom fusion | bytes 4227072 | tf_op jit(solution)/shard_map/while/body/eval_jaxpr/jit(_take)/gather | solution.py:17
  90.9 29.5 %gather_fusion = bf16[8192,128]{1,0:T(8,128)(2,1)} fusion(bf16[12289,128]{1,0:T(8,128)(2,1)S(1)} %get-tuple-element.121, s32[8192]{0:T(1024)S(1)} %broadcast_clamp_fusion.2), kind=kCustom, calls=%fused_computation.1.clone.clone.1 | custom fusion | bytes 4227072 | tf_op jit(solution)/shard_map/while/body/eval_jaxpr/jit(_take)/gather | solution.py:17
  120.4 7.7 convolution_add_fusion.2
  129.1 29.5 %gather_fusion = bf16[8192,128]{1,0:T(8,128)(2,1)} fusion(bf16[12289,128]{1,0:T(8,128)(2,1)S(1)} %get-tuple-element.121, s32[8192]{0:T(1024)S(1)} %broadcast_clamp_fusion.2), kind=kCustom, calls=%fused_computation.1.clone.clone.1 | custom fusion | bytes 4227072 | tf_op jit(solution)/shard_map/while/body/eval_jaxpr/jit(_take)/gather | solution.py:17
  158.6 7.7 convolution_add_fusion.2
  167.3 29.5 %gather_fusion = bf16[8192,128]{1,0:T(8,128)(2,1)} fusion(bf16[12289,128]{1,0:T(8,128)(2,1)S(1)} %get-tuple-element.121, s32[8192]{0:T(1024)S(1)} %broadcast_clamp_fusion.2), kind=kCustom, calls=%fused_computation.1.clone.clone.1 | custom fusion | bytes 4227072 | tf_op jit(solution)/shard_map/while/body/eval_jaxpr/jit(_take)/gather | solution.py:17
  205.5 29.5 %gather_fusion = bf16[8192,128]{1,0:T(8,128)(2,1)} fusion(bf16[12289,128]{1,0:T(8,128)(2,1)S(1)} %get-tuple-element.121, s32[8192]{0:T(1024)S(1)} %broadcast_clamp_fusion.2), kind=kCustom, calls=%fused_computation.1.clone.clone.1 | custom fusion | bytes 4227072 | tf_op jit(solution)/shard_map/while/body/eval_jaxpr/jit(_take)/gather | solution.py:17
  243.6 29.5 %gather_fusion = bf16[8192,128]{1,0:T(8,128)(2,1)} fusion(bf16[12289,128]{1,0:T(8,128)(2,1)S(1)} %get-tuple-element.121, s32[8192]{0:T(1024)S(1)} %broadcast_clamp_fusion.2), kind=kCustom, calls=%fused_computation.1.clone.clone.1 | custom fusion | bytes 4227072 | tf_op jit(solution)/shard_map/while/body/eval_jaxpr/jit(_take)/gather | solution.py:17
  281.8 29.5 %gather_fusion = bf16[8192,128]{1,0:T(8,128)(2,1)} fusion(bf16[12289,128]{1,0:T(8,128)(2,1)S(1)} %get-tuple-element.121, s32[8192]{0:T(1024)S(1)} %broadcast_clamp_fusion.2), kind=kCustom, calls=%fused_computation.1.clone.clone.1 | custom fusion | bytes 4227072 | tf_op jit(solution)/shard_map/while/body/eval_jaxpr/jit(_take)/gather | solution.py:17
  311.3 7.7 convolution_add_fusion.2
  320.0 29.5 %gather_fusion = bf16[8192,128]{1,0:T(8,128)(2,1)} fusion(bf16[12289,128]{1,0:T(8,128)(2,1)S(1)} %get-tuple-element.121, s32[8192]{0:T(1024)S(1)} %broadcast_clamp_fusion.2), kind=kCustom, calls=%fused_computation.1.clone.clone.1 | custom fusion | bytes 4227072 | tf_op jit(solution)/shard_map/while/body/eval_jaxpr/jit(_take)/gather | solution.py:17
  358.2 29.5 %gather_fusion = bf16[8192,128]{1,0:T(8,128)(2,1)} fusion(bf16[12289,128]{1,0:T(8,128)(2,1)S(1)} %get-tuple-element.121, s32[8192]{0:T(1024)S(1)} %broadcast_clamp_fusion.2), kind=kCustom, calls=%fused_computation.1.clone.clone.1 | custom fusion | bytes 4227072 | tf_op jit(solution)/shard_map/while/body/eval_jaxpr/jit(_take)/gather | solution.py:17
  396.4 29.5 %gather_fusion = bf16[8192,128]{1,0:T(8,128)(2,1)} fusion(bf16[12289,128]{1,0:T(8,128)(2,1)S(1)} %get-tuple-element.121, s32[8192]{0:T(1024)S(1)} %broadcast_clamp_fusion.2), kind=kCustom, calls=%fused_computation.1.clone.clone.1 | custom fusion | bytes 4227072 | tf_op jit(solution)/shard_map/while/body/eval_jaxpr/jit(_take)/gather | solution.py:17
  425.9 7.7 convolution_add_fusion.2
  434.6 29.5 %gather_fusion = bf16[8192,128]{1,0:T(8,128)(2,1)} fusion(bf16[12289,128]{1,0:T(8,128)(2,1)S(1)} %get-tuple-element.121, s32[8192]{0:T(1024)S(1)} %broadcast_clamp_fusion.2), kind=kCustom, calls=%fused_computation.1.clone.clone.1 | custom fusion | bytes 4227072 | tf_op jit(solution)/shard_map/while/body/eval_jaxpr/jit(_take)/gather | solution.py:17
  464.1 7.7 convolution_add_fusion.2
  472.7 29.5 %gather_fusion = bf16[8192,128]{1,0:T(8,128)(2,1)} fusion(bf16[12289,128]{1,0:T(8,128)(2,1)S(1)} %get-tuple-element.121, s32[8192]{0:T(1024)S(1)} %broadcast_clamp_fusion.2), kind=kCustom, calls=%fused_computation.1.clone.clone.1 | custom fusion | bytes 4227072 | tf_op jit(solution)/shard_map/while/body/eval_jaxpr/jit(_take)/gather | solution.py:17
  502.2 7.7 convolution_add_fusion.2
  510.9 29.5 %gather_fusion = bf16[8192,128]{1,0:T(8,128)(2,1)} fusion(bf16[12289,128]{1,0:T(8,128)(2,1)S(1)} %get-tuple-element.121, s32[8192]{0:T(1024)S(1)} %broadcast_clamp_fusion.2), kind=kCustom, calls=%fused_computation.1.clone.clone.1 | custom fusion | bytes 4227072 | tf_op jit(solution)/shard_map/while/body/eval_jaxpr/jit(_take)/gather | solution.py:17
  540.4 7.7 convolution_add_fusion.2
  549.1 29.5 %gather_fusion = bf16[8192,128]{1,0:T(8,128)(2,1)} fusion(bf16[12289,128]{1,0:T(8,128)(2,1)S(1)} %get-tuple-element.121, s32[8192]{0:T(1024)S(1)} %broadcast_clamp_fusion.2), kind=kCustom, calls=%fused_computation.1.clone.clone.1 | custom fusion | bytes 4227072 | tf_op jit(solution)/shard_map/while/body/eval_jaxpr/jit(_take)/gather | solution.py:17
  578.6 7.7 convolution_add_fusion.2
  587.3 29.5 %gather_fusion = bf16[8192,128]{1,0:T(8,128)(2,1)} fusion(bf16[12289,128]{1,0:T(8,128)(2,1)S(1)} %get-tuple-element.121, s32[8192]{0:T(1024)S(1)} %broadcast_clamp_fusion.2), kind=kCustom, calls=%fused_computation.1.clone.clone.1 | custom fusion | bytes 4227072 | tf_op jit(solution)/shard_map/while/body/eval_jaxpr/jit(_take)/gather | solution.py:17
  616.8 7.7 convolution_add_fusion.2
  625.5 29.5 %gather_fusion = bf16[8192,128]{1,0:T(8,128)(2,1)} fusion(bf16[12289,128]{1,0:T(8,128)(2,1)S(1)} %get-tuple-element.121, s32[8192]{0:T(1024)S(1)} %broadcast_clamp_fusion.2), kind=kCustom, calls=%fused_computation.1.clone.clone.1 | custom fusion | bytes 4227072 | tf_op jit(solution)/shard_map/while/body/eval_jaxpr/jit(_take)/gather | solution.py:17
  655.0 7.7 convolution_add_fusion.2
  663.7 29.5 %gather_fusion = bf16[8192,128]{1,0:T(8,128)(2,1)} fusion(bf16[12289,128]{1,0:T(8,128)(2,1)S(1)} %get-tuple-element.121, s32[8192]{0:T(1024)S(1)} %broadcast_clamp_fusion.2), kind=kCustom, calls=%fused_computation.1.clone.clone.1 | custom fusion | bytes 4227072 | tf_op jit(solution)/shard_map/while/body/eval_jaxpr/jit(_take)/gather | solution.py:17
  701.8 29.5 %gather_fusion = bf16[8192,128]{1,0:T(8,128)(2,1)} fusion(bf16[12289,128]{1,0:T(8,128)(2,1)S(1)} %get-tuple-element.121, s32[8192]{0:T(1024)S(1)} %broadcast_clamp_fusion.2), kind=kCustom, calls=%fused_computation.1.clone.clone.1 | custom fusion | bytes 4227072 | tf_op jit(solution)/shard_map/while/body/eval_jaxpr/jit(_take)/gather | solution.py:17
  731.3 7.7 convolution_add_fusion.2
  740.0 29.5 %gather_fusion = bf16[8192,128]{1,0:T(8,128)(2,1)} fusion(bf16[12289,128]{1,0:T(8,128)(2,1)S(1)} %get-tuple-element.121, s32[8192]{0:T(1024)S(1)} %broadcast_clamp_fusion.2), kind=kCustom, calls=%fused_computation.1.clone.clone.1 | custom fusion | bytes 4227072 | tf_op jit(solution)/shard_map/while/body/eval_jaxpr/jit(_take)/gather | solution.py:17
  778.2 29.5 %gather_fusion = bf16[8192,128]{1,0:T(8,128)(2,1)} fusion(bf16[12289,128]{1,0:T(8,128)(2,1)S(1)} %get-tuple-element.121, s32[8192]{0:T(1024)S(1)} %broadcast_clamp_fusion.2), kind=kCustom, calls=%fused_computation.1.clone.clone.1 | custom fusion | bytes 4227072 | tf_op jit(solution)/shard_map/while/body/eval_jaxpr/jit(_take)/gather | solution.py:17
  807.7 7.7 convolution_add_fusion.2
  816.4 29.5 %gather_fusion = bf16[8192,128]{1,0:T(8,128)(2,1)} fusion(bf16[12289,128]{1,0:T(8,128)(2,1)S(1)} %get-tuple-element.121, s32[8192]{0:T(1024)S(1)} %broadcast_clamp_fusion.2), kind=kCustom, calls=%fused_computation.1.clone.clone.1 | custom fusion | bytes 4227072 | tf_op jit(solution)/shard_map/while/body/eval_jaxpr/jit(_take)/gather | solution.py:17
  854.6 29.5 %gather_fusion = bf16[8192,128]{1,0:T(8,128)(2,1)} fusion(bf16[12289,128]{1,0:T(8,128)(2,1)S(1)} %get-tuple-element.121, s32[8192]{0:T(1024)S(1)} %broadcast_clamp_fusion.2), kind=kCustom, calls=%fused_computation.1.clone.clone.1 | custom fusion | bytes 4227072 | tf_op jit(solution)/shard_map/while/body/eval_jaxpr/jit(_take)/gather | solution.py:17
  884.1 7.7 convolution_add_fusion.2
  892.8 29.5 %gather_fusion = bf16[8192,128]{1,0:T(8,128)(2,1)} fusion(bf16[12289,128]{1,0:T(8,128)(2,1)S(1)} %get-tuple-element.121, s32[8192]{0:T(1024)S(1)} %broadcast_clamp_fusion.2), kind=kCustom, calls=%fused_computation.1.clone.clone.1 | custom fusion | bytes 4227072 | tf_op jit(solution)/shard_map/while/body/eval_jaxpr/jit(_take)/gather | solution.py:17
  922.3 7.7 convolution_add_fusion.2
  930.9 29.5 %gather_fusion = bf16[8192,128]{1,0:T(8,128)(2,1)} fusion(bf16[12289,128]{1,0:T(8,128)(2,1)S(1)} %get-tuple-element.121, s32[8192]{0:T(1024)S(1)} %broadcast_clamp_fusion.2), kind=kCustom, calls=%fused_computation.1.clone.clone.1 | custom fusion | bytes 4227072 | tf_op jit(solution)/shard_map/while/body/eval_jaxpr/jit(_take)/gather | solution.py:17
  969.1 29.5 %gather_fusion = bf16[8192,128]{1,0:T(8,128)(2,1)} fusion(bf16[12289,128]{1,0:T(8,128)(2,1)S(1)} %get-tuple-element.121, s32[8192]{0:T(1024)S(1)} %broadcast_clamp_fusion.2), kind=kCustom, calls=%fused_computation.1.clone.clone.1 | custom fusion | bytes 4227072 | tf_op jit(solution)/shard_map/while/body/eval_jaxpr/jit(_take)/gather | solution.py:17
  1007.3 29.5 %gather_fusion = bf16[8192,128]{1,0:T(8,128)(2,1)} fusion(bf16[12289,128]{1,0:T(8,128)(2,1)S(1)} %get-tuple-element.121, s32[8192]{0:T(1024)S(1)} %broadcast_clamp_fusion.2), kind=kCustom, calls=%fused_computation.1.clone.clone.1 | custom fusion | bytes 4227072 | tf_op jit(solution)/shard_map/while/body/eval_jaxpr/jit(_take)/gather | solution.py:17
  1036.8 7.7 convolution_add_fusion.2
  1045.5 29.5 %gather_fusion = bf16[8192,128]{1,0:T(8,128)(2,1)} fusion(bf16[12289,128]{1,0:T(8,128)(2,1)S(1)} %get-tuple-element.121, s32[8192]{0:T(1024)S(1)} %broadcast_clamp_fusion.2), kind=kCustom, calls=%fused_computation.1.clone.clone.1 | custom fusion | bytes 4227072 | tf_op jit(solution)/shard_map/while/body/eval_jaxpr/jit(_take)/gather | solution.py:17
  1095.5 43.3 %gather_fusion.1 = bf16[12288,128]{1,0:T(8,128)(2,1)} fusion(bf16[8193,128]{1,0:T(8,128)(2,1)S(1)} %concatenate.7, s32[12288]{0:T(1024)S(1)} %fusion.7), kind=kCustom, calls=%fused_computation.3 | custom fusion | bytes 6340608 | tf_op jit(solution)/shard_map/jit(_take)/gather | solution.py:44
  1152.2 34.4 %all-to-all-done = bf16[8,1536,128]{2,1,0:T(8,128)(2,1)S(1)} async-done(((bf16[8,1536,128]{2,1,0:T(8,128)(2,1)}), bf16[8,1536,128]{2,1,0:T(8,128)(2,1)S(1)}, u32[]{:S(2)}, u32[]{:S(2)}) %all-to-all-start) | async-done | bytes 3145760 | tf_op jit(solution)/shard_map/all_to_all | solution.py:45
  1186.6 29.5 %gather_fusion.2 = bf16[8192,128]{1,0:T(8,128)(2,1)} fusion(bf16[12288,128]{1,0:T(8,128)(2,1)S(1)} %bitcast.20, s32[8192]{0:T(1024)S(1)} %fusion.8), kind=kCustom, calls=%fused_computation.4 | custom fusion | bytes 4227072 | tf_op jit(solution)/shard_map/jit(_take)/gather | solution.py:52
  (139 shorter events, 173.8 us)
Async XLA Ops:
  0.0 14.1 %copy-start.1 = (bf16[8192,128]{1,0:T(8,128)(2,1)S(1)}, bf16[8192,128]{1,0:T(8,128)(2,1)}, u32[]{:S(2)}) copy-start(bf16[8192,128]{1,0:T(8,128)(2,1)} %param.13) | copy-start | bytes 6291460
  0.0 14.1 %copy-start.6 = (s32[2048]{0:T(1024)S(1)}, s32[2048]{0:T(1024)}, u32[]{:S(2)}) copy-start(s32[2048]{0:T(1024)} %param.15) | copy-start | bytes 24580
  9.4 13.2 %copy-start.4 = (s32[12288]{0:T(1024)S(1)}, s32[12288]{0:T(1024)}, u32[]{:S(2)}) copy-start(s32[12288]{0:T(1024)} %param.17) | copy-start | bytes 147460
  9.4 13.2 %copy-start.3 = (bf16[27,128,32]{1,2,0:T(8,128)(2,1)S(1)}, bf16[27,128,32]{1,2,0:T(8,128)(2,1)}, u32[]{:S(2)}) copy-start(bf16[27,128,32]{1,2,0:T(8,128)(2,1)} %param.19) | copy-start | bytes 663556
  9.4 33.0 %collective-permute-start = (bf16[2048,128]{1,0:T(8,128)(2,1)S(1)}, bf16[2048,128]{1,0:T(8,128)(2,1)}, u32[]{:S(2)}, u32[]{:S(2)}) collective-permute-start(bf16[2048,128]{1,0:T(8,128)(2,1)S(1)} %broadcast_select_fusion.3), channel_id=1, source_target_pairs={{0,4},{4,8},{8,12},{12,16},{16,20},{20,24},{24,28},{1,5},{5,9},{9,... | collective-permute-start | bytes 1572872 | tf_op jit(solution)/shard_map/ppermute | solution.py:10
  20.6 21.8 %collective-permute-start.1 = (bf16[2048,128]{1,0:T(8,128)(2,1)S(1)}, bf16[2048,128]{1,0:T(8,128)(2,1)}, u32[]{:S(2)}, u32[]{:S(2)}) collective-permute-start(bf16[2048,128]{1,0:T(8,128)(2,1)S(1)} %broadcast_select_fusion.2), channel_id=1, source_target_pairs={{4,0},{8,4},{12,8},{16,12},{20,16},{24,20},{28,24},{5,1},{9,5},{13... | collective-permute-start | bytes 1572872 | tf_op jit(solution)/shard_map/ppermute | solution.py:10
  1082.7 7.7 copy-start.2
  1086.2 4.2 copy-start
  1086.2 4.2 copy-start.7
  1086.2 4.2 copy-start.8
  1146.0 6.2 copy-start.5
  1146.0 40.6 %all-to-all-start = ((bf16[8,1536,128]{2,1,0:T(8,128)(2,1)}), bf16[8,1536,128]{2,1,0:T(8,128)(2,1)S(1)}, u32[]{:S(2)}, u32[]{:S(2)}) async-start(bf16[8,1536,128]{2,1,0:T(8,128)(2,1)} %broadcast_select_fusion), calls=%async_computation | async-start | bytes 6291456 | tf_op jit(solution)/shard_map/all_to_all | solution.py:45
where the time goes:
time: 1230 us; the launch traced here: 1220 us
  local copies, waits for them, and re-layouts  883 us (72%)
  matrix products  206 us (17%)
  other arithmetic  66.3 us (5%)
  waiting for transfers between devices  34.4 us (3%)
  blocking collectives  19.7 us (2%)
  starting transfers between devices  12.8 us (1%)
    gather x27, local copies, waits for them, and re-layouts, advance(): picked = jnp.take(extended, column, axis=0)  796 us
    dot_general x27, matrix products, advance(): jnp.dot(picked, weight_mat, preferred_element_type=jnp.float32)  206 us
    gather x1, local copies, waits for them, and re-layouts, body(): outbox = jnp.take(padded, send_slot, axis=0)  43.3 us
    all_to_all x1, waiting for transfers between devices, body(): lax.all_to_all(outbox.reshape(slab_count, capacity, channels), 'brick', s...  34.4 us
    gather x1, local copies, waits for them, and re-layouts, body(): jnp.take(arrived.reshape(slab_count * capacity, channels), recv_slot, axi...  29.5 us
    select_n x27, other arithmetic, advance(): picked = jnp.take(extended, column, axis=0)  26.9 us
  transfers between devices with their start and end apart: 3, of which 1 were waited for; matrix products, arithmetic and copies ran while one was open for 1% of the time, Pallas kernels for 0%

commit v1 on v0

--- a/solution.py
+++ b/solution.py
@@ -1,7 +1,13 @@
+import functools
+
 import jax
 import jax.numpy as jnp
 from jax import lax
+from jax.experimental import pallas as pl
+from jax.experimental.pallas import tpu as pltpu
 from jax.sharding import PartitionSpec as P
+
+BLOCK = 256
 
 
 def shifted(block, axis, distance):
@@ -10,15 +16,95 @@
     return lax.ppermute(block, axis, route)
 
 
-def convolve(extended, columns, kernel):
+def conv_kernel(
+    nb_ref, feat_ref, low_ref, up_ref, w_ref, gain_ref, shift_ref, out_ref, tab_ref, buf_a, buf_b, acc_ref
+):
+    step = pl.program_id(0)
+    rows, channels = feat_ref.shape
+    halo = low_ref.shape[0]
+    offsets, block = nb_ref.shape
+    table = tab_ref.reshape(tab_ref.shape[0], 1, channels)
 
-    def advance(summed, packed):
-        column, weight_mat = packed
-        picked = jnp.take(extended, column, axis=0)
-        return (summed + jnp.dot(picked, weight_mat, preferred_element_type=jnp.float32), None)
+    @pl.when(step == 0)
+    def _():
+        chunk = 256
+        for src, start in ((feat_ref, 0), (low_ref, rows), (up_ref, rows + halo)):
 
-    initial = jnp.zeros((columns.shape[1], kernel.shape[2]), jnp.float32)
-    return lax.scan(advance, initial, (columns, kernel))[0]
+            @pl.loop(0, src.shape[0] // chunk)
+            def _(i, src=src, start=start):
+                at = pl.multiple_of(i * chunk, chunk)
+                tab_ref[pl.ds(start + at, chunk), :] = src[pl.ds(at, chunk), :].astype(jnp.float32)
+
+        tab_ref[pl.ds(rows + 2 * halo, 8), :] = jnp.zeros((8, channels), jnp.float32)
+
+    def gather(first, buf, count=2):
+        for j in range(count):
+            for v in range(block):
+                buf[pl.ds(v, 1), pl.ds(j * channels, channels)] = table[nb_ref[first + j, v]]
+
+    def multiply(first, buf, count=2):
+        lhs = buf[:, : count * channels].astype(jnp.bfloat16)
+        at = pl.multiple_of(first * channels, channels)
+        rhs = w_ref[pl.ds(at, count * channels), :]
+        acc_ref[...] += jnp.dot(lhs, rhs, preferred_element_type=jnp.float32)
+
+    acc_ref[...] = jnp.zeros_like(acc_ref)
+    pairs = offsets // 2
+    gather(0, buf_a)
+
+    @pl.loop(0, (pairs - 1) // 2)
+    def _(p):
+        first = p * 4
+        gather(first + 2, buf_b)
+        multiply(first, buf_a)
+        gather(first + 4, buf_a)
+        multiply(first + 2, buf_b)
+
+    gather(offsets - 1, buf_b, 1)
+    multiply(offsets - 3, buf_a)
+    multiply(offsets - 1, buf_b, 1)
+
+    summed = acc_ref[...]
+    centered = summed - jnp.mean(summed, axis=-1, keepdims=True)
+    spread_sq = jnp.mean(centered * centered, axis=-1, keepdims=True)
+    normed = centered * lax.rsqrt(spread_sq + 1e-05) * gain_ref[...] + shift_ref[...]
+    own = feat_ref[pl.ds(pl.multiple_of(step * block, block), block), :].astype(jnp.float32)
+    out_ref[...] = (own + normed / (1.0 + jnp.exp(-normed))).astype(jnp.bfloat16)
+
+
+def conv_block(features, from_lower, from_upper, columns, weights, gain, shift):
+    rows, channels = features.shape
+    halo = from_lower.shape[0]
+    offsets = columns.shape[0]
+    block = BLOCK
+    whole = pl.BlockSpec(memory_space=pltpu.VMEM)
+    return pl.pallas_call(
+        conv_kernel,
+        grid=(rows // block,),
+        out_shape=jax.ShapeDtypeStruct((rows, channels), jnp.bfloat16),
+        in_specs=[
+            pl.BlockSpec((offsets, block), lambda i: (0, i), memory_space=pltpu.SMEM),
+            whole,
+            whole,
+            whole,
+            whole,
+            whole,
+            whole,
+        ],
+        out_specs=pl.BlockSpec((block, channels), lambda i: (i, 0)),
+        scratch_shapes=[
+            pltpu.VMEM((rows + 2 * halo + 8, channels), jnp.float32),
+            pltpu.VMEM((block, 2 * channels), jnp.float32),
+            pltpu.VMEM((block, 2 * channels), jnp.float32),
+            pltpu.VMEM((block, channels), jnp.float32),
+        ],
+        compiler_params=pltpu.CompilerParams(vmem_limit_bytes=48 * 1024 * 1024),
+        cost_estimate=pl.CostEstimate(
+            flops=2 * rows * offsets * channels * channels,
+            bytes_accessed=8 * rows * channels,
+            transcendentals=rows * channels,
+        ),
+    )(columns, features, from_lower, from_upper, weights, gain, shift)
 
 
 def body(
@@ -31,13 +117,15 @@
     downward = jnp.take(features, send_low, axis=0)
     from_lower = shifted(upward, "brick", 1)
     from_upper = shifted(downward, "brick", -1)
-    columns = neighbors.T
-    extended = jnp.concatenate([features, from_lower, from_upper, zero_row], axis=0)
-    summed = convolve(extended, columns, weights)
-    centered = summed - jnp.mean(summed, axis=-1, keepdims=True)
-    spread_sq = jnp.mean(centered * centered, axis=-1, keepdims=True)
-    normed = centered * lax.rsqrt(spread_sq + 1e-05) * norm_gain + norm_shift
-    blended = (features.astype(jnp.float32) + jax.nn.silu(normed)).astype(jnp.bfloat16)
+    blended = conv_block(
+        features,
+        from_lower,
+        from_upper,
+        neighbors.T,
+        weights.reshape(-1, channels),
+        norm_gain.reshape(1, channels),
+        norm_shift.reshape(1, channels),
+    )
     slab_count = lax.axis_size("brick")
     capacity = send_slot.shape[0] // slab_count
     padded = jnp.concatenate([blended, zero_row], axis=0)

time: 1230 us -> 445 us (0.36)
  local copies, waits for them, and re-layouts: 883 us -> 88.8 us
  Pallas kernels: 0 us -> 268 us
  matrix products: 206 us -> 0 us
  other arithmetic: 66.3 us -> 17.5 us
    gather x27 -> x0, local copies, waits for them, and re-layouts: 796 us -> none  [advance(): picked = jnp.take(extended, column, axis=0)]
    pallas_call x0 -> x1, Pallas kernels: none -> 268 us  [conv_block(): pl.pallas_call(conv_kernel, grid=(rows // block,), out_shape=jax.ShapeDty...]
    dot_general x27 -> x0, matrix products: 206 us -> none  [advance(): jnp.dot(picked, weight_mat, preferred_element_type=jnp.float32)]
    select_n x27 -> x0, other arithmetic: 26.9 us -> none  [advance(): picked = jnp.take(extended, column, axis=0)]
  transfers between devices with their start and end apart: 3 -> 3, of which waited for: 1 -> 1; matrix products, arithmetic and copies ran while one was open for 1% -> 2% of each run, Pallas kernels for 0% -> 0%
where the time goes in v1:
time: 445 us; the launch traced here: 441 us
  Pallas kernels  268 us (60%)
  local copies, waits for them, and re-layouts  88.8 us (20%)
  waiting for transfers between devices  34.4 us (8%)
  blocking collectives  18.9 us (4%)
  other arithmetic  17.5 us (4%)
  starting transfers between devices  13.4 us (3%)
    pallas_call x1, Pallas kernels, conv_block(): pl.pallas_call(conv_kernel, grid=(rows // block,), out_shape=jax.ShapeDty...  268 us
    gather x1, local copies, waits for them, and re-layouts, body(): outbox = jnp.take(padded, send_slot, axis=0)  43.3 us
    all_to_all x1, waiting for transfers between devices, body(): lax.all_to_all(outbox.reshape(slab_count, capacity, channels), 'brick', s...  34.4 us
    gather x1, local copies, waits for them, and re-layouts, body(): jnp.take(arrived.reshape(slab_count * capacity, channels), recv_slot, axi...  29.5 us
    all_gather x1, blocking collectives, body(): weights = lax.all_gather(kernel, 'grp', axis=2, tiled=True)  18.9 us
  transfers between devices with their start and end apart: 3, of which 1 were waited for; matrix products, arithmetic and copies ran while one was open for 2% of the time, Pallas kernels for 0%

profile of v1, /device:TPU:1, one launch (start us, length us, event | category | flops | bytes accessed | tf_op | source)
XLA Modules:
  0.0 441.1 jit_solution(690459394126506339)
XLA Ops:
  0.0 0.7 fusion.2
  0.7 0.7 compare_and_fusion.3
  1.4 0.0 copy-start.7
  1.4 0.0 copy-start.3
  1.4 7.6 %gather_fusion.2 = bf16[2048,128]{1,0:T(8,128)(2,1)S(1)} fusion(bf16[8192,128]{1,0:T(8,128)(2,1)} %feat_ref.1, s32[2048]{0:T(1024)S(1)} %fusion.2), kind=kCustom, calls=%fused_computation.clone | custom fusion | bytes 1056768 | tf_op jit(solution)/shard_map/jit(_take)/gather | solution.py:116
  9.0 1.1 broadcast_select_fusion.3
  10.2 4.5 %collective-permute-start = (bf16[2048,128]{1,0:T(8,128)(2,1)}, bf16[2048,128]{1,0:T(8,128)(2,1)S(1)}, u32[]{:S(2)}, u32[]{:S(2)}) collective-permute-start(bf16[2048,128]{1,0:T(8,128)(2,1)} %broadcast_select_fusion.3), channel_id=1, source_target_pairs={{0,4},{4,8},{8,12},{12,16},{16,20},{20,24},{24,28},{1,5},{5,9},{9,... | collective-permute-start | bytes 1572872 | tf_op jit(solution)/shard_map/ppermute | solution.py:16
  14.7 0.0 copy-done.7
  14.7 0.0 copy-done.3
  14.7 0.0 copy-start.5
  14.7 0.0 copy-start.4
  14.7 6.2 %gather_fusion.3 = bf16[2048,128]{1,0:T(8,128)(2,1)S(1)} fusion(bf16[8192,128]{1,0:T(8,128)(2,1)S(1)} %copy-done.3, s32[2048]{0:T(1024)S(1)} %fusion.3), kind=kCustom, calls=%fused_computation.1.clone | custom fusion | bytes 1056768 | tf_op jit(solution)/shard_map/jit(_take)/gather | solution.py:117
  20.9 0.0 copy-start
  20.9 0.0 copy-start.1
  21.0 0.0 copy-start.2
  21.0 1.1 broadcast_select_fusion.2
  22.1 1.9 collective-permute-start.1
  24.0 0.0 copy-done.5
  24.1 0.0 copy-done.4
  24.1 18.9 %all_gather.3 = bf16[27,128,128]{1,2,0:T(8,128)(2,1)} all-gather(bf16[27,128,32]{1,2,0:T(8,128)(2,1)S(1)} %copy-done.4), channel_id=1, replica_groups=mesh['brick'=8,'grp'=4] {'grp'}, dimensions={2}, use_global_device_ids=true | all-gather | bytes 1105920 | tf_op jit(solution)/shard_map/all_gather | solution.py:115
  43.0 1.9 copy.10
  44.9 0.1 broadcast_in_dim.37
  45.0 0.0 collective-permute-done.low_ref
  45.0 0.0 collective-permute-done.1.up_ref
  45.0 0.0 copy-done
  45.0 0.0 copy-done.1
  45.0 0.0 copy-done.2
  45.0 267.8 %shard_map.91 = bf16[8192,128]{1,0:T(8,128)(2,1)S(1)} custom-call(s32[27,8192]{1,0:T(8,128)S(1)} %bitcast.7, bf16[8192,128]{1,0:T(8,128)(2,1)} %feat_ref.1, bf16[2048,128]{1,0:T(8,128)(2,1)S(1)} %collective-permute-done.low_ref, bf16[2048,128]{1,0:T(8,128)(2,1)S(1)} %collective-permute-done.1.up_ref, bf16[3456,128]{1,0:T(8,128)(2,1)S(1)} %bitcast.6, ...), custom_call_target="tpu_custom_call" | custom-call | flops 7247757312 | bytes 8388608 | tf_op jit(solution)/shard_map/pallas_call | solution.py:81
  312.9 0.2 concatenate.3
  313.1 43.3 %gather_fusion = bf16[12288,128]{1,0:T(8,128)(2,1)} fusion(bf16[8193,128]{1,0:T(8,128)(2,1)S(1)} %concatenate.3, s32[12288]{0:T(1024)S(1)} %fusion), kind=kCustom, calls=%fused_computation.2 | custom fusion | bytes 6340608 | tf_op jit(solution)/shard_map/jit(_take)/gather | solution.py:132
  356.4 7.2 %broadcast_select_fusion = bf16[8,1536,128]{2,1,0:T(8,128)(2,1)} fusion(bf16[8,1536,128]{2,1,0:T(8,128)(2,1)} %bitcast.11, pred[8,1536]{1,0:T(8,128)(4,1)S(1)} %broadcast_in_dim.37), kind=kLoop, calls=%fused_computation.4 | loop fusion | flops 1572864 | bytes 6303744 | tf_op jit(solution)/shard_map/jit(_take)/select_n | solution.py:132
  363.6 0.0 copy-start.6
  363.6 7.0 %all-to-all-start = ((bf16[8,1536,128]{2,1,0:T(8,128)(2,1)}), bf16[8,1536,128]{2,1,0:T(8,128)(2,1)S(1)}, u32[]{:S(2)}, u32[]{:S(2)}) async-start(bf16[8,1536,128]{2,1,0:T(8,128)(2,1)} %broadcast_select_fusion), calls=%async_computation | async-start | bytes 6291456 | tf_op jit(solution)/shard_map/all_to_all | solution.py:133
  370.6 0.0 copy-done.6
  370.6 34.4 %all-to-all-done = bf16[8,1536,128]{2,1,0:T(8,128)(2,1)S(1)} async-done(((bf16[8,1536,128]{2,1,0:T(8,128)(2,1)}), bf16[8,1536,128]{2,1,0:T(8,128)(2,1)S(1)}, u32[]{:S(2)}, u32[]{:S(2)}) %all-to-all-start) | async-done | bytes 3145760 | tf_op jit(solution)/shard_map/all_to_all | solution.py:133
  405.0 29.5 %gather_fusion.1 = bf16[8192,128]{1,0:T(8,128)(2,1)} fusion(bf16[12288,128]{1,0:T(8,128)(2,1)S(1)} %bitcast.10, s32[8192]{0:T(1024)S(1)} %fusion.1), kind=kCustom, calls=%fused_computation.3 | custom fusion | bytes 4227072 | tf_op jit(solution)/shard_map/jit(_take)/gather | solution.py:140
  434.5 6.6 %broadcast_select_fusion.1 = bf16[8192,128]{1,0:T(8,128)(2,1)} fusion(bf16[8192,128]{1,0:T(8,128)(2,1)} %gather_fusion.1, pred[8192]{0:T(1024)(128)(4,1)S(1)} %compare_and_fusion.1), kind=kLoop, calls=%fused_computation.5 | loop fusion | flops 1048576 | bytes 4202496 | tf_op jit(solution)/shard_map/jit(_take)/select_n | solution.py:140
  (6 shorter events, 0.1 us)
Async XLA Ops:
  1.4 13.3 %copy-start.7 = (s32[2048]{0:T(1024)S(1)}, s32[2048]{0:T(1024)}, u32[]{:S(2)}) copy-start(s32[2048]{0:T(1024)} %param.13) | copy-start | bytes 24580
  1.4 13.3 %copy-start.3 = (bf16[8192,128]{1,0:T(8,128)(2,1)S(1)}, bf16[8192,128]{1,0:T(8,128)(2,1)}, u32[]{:S(2)}) copy-start(bf16[8192,128]{1,0:T(8,128)(2,1)} %feat_ref.1) | copy-start | bytes 6291460
  10.2 34.8 %collective-permute-start = (bf16[2048,128]{1,0:T(8,128)(2,1)}, bf16[2048,128]{1,0:T(8,128)(2,1)S(1)}, u32[]{:S(2)}, u32[]{:S(2)}) collective-permute-start(bf16[2048,128]{1,0:T(8,128)(2,1)} %broadcast_select_fusion.3), channel_id=1, source_target_pairs={{0,4},{4,8},{8,12},{12,16},{16,20},{20,24},{24,28},{1,5},{5,9},{9,... | collective-permute-start | bytes 1572872 | tf_op jit(solution)/shard_map/ppermute | solution.py:16
  14.7 9.3 %copy-start.5 = (s32[12288]{0:T(1024)S(1)}, s32[12288]{0:T(1024)}, u32[]{:S(2)}) copy-start(s32[12288]{0:T(1024)} %param.15) | copy-start | bytes 147460
  14.7 9.3 %copy-start.4 = (bf16[27,128,32]{1,2,0:T(8,128)(2,1)S(1)}, bf16[27,128,32]{1,2,0:T(8,128)(2,1)}, u32[]{:S(2)}) copy-start(bf16[27,128,32]{1,2,0:T(8,128)(2,1)} %param.17) | copy-start | bytes 663556
  20.9 24.1 %copy-start = (s32[8192,27]{0,1:T(8,128)S(1)}, s32[8192,27]{0,1:T(8,128)}, u32[]{:S(2)}) copy-start(s32[8192,27]{0,1:T(8,128)} %param.12) | copy-start | bytes 2654212
  20.9 24.1 %copy-start.1 = (f32[128]{0:T(128)S(1)}, f32[128]{0:T(128)}, u32[]{:S(2)}) copy-start(f32[128]{0:T(128)} %param.18) | copy-start | bytes 1540
  21.0 24.1 %copy-start.2 = (f32[128]{0:T(128)S(1)}, f32[128]{0:T(128)}, u32[]{:S(2)}) copy-start(f32[128]{0:T(128)} %param.19) | copy-start | bytes 1540
  22.1 22.9 %collective-permute-start.1 = (bf16[2048,128]{1,0:T(8,128)(2,1)}, bf16[2048,128]{1,0:T(8,128)(2,1)S(1)}, u32[]{:S(2)}, u32[]{:S(2)}) collective-permute-start(bf16[2048,128]{1,0:T(8,128)(2,1)} %broadcast_select_fusion.2), channel_id=1, source_target_pairs={{4,0},{8,4},{12,8},{16,12},{20,16},{24,20},{28,24},{5,1},{9,5},{13... | collective-permute-start | bytes 1572872 | tf_op jit(solution)/shard_map/ppermute | solution.py:16
  363.6 7.0 %copy-start.6 = (s32[8192]{0:T(1024)S(1)}, s32[8192]{0:T(1024)}, u32[]{:S(2)}) copy-start(s32[8192]{0:T(1024)} %param.16) | copy-start | bytes 98308
  363.6 41.4 %all-to-all-start = ((bf16[8,1536,128]{2,1,0:T(8,128)(2,1)}), bf16[8,1536,128]{2,1,0:T(8,128)(2,1)S(1)}, u32[]{:S(2)}, u32[]{:S(2)}) async-start(bf16[8,1536,128]{2,1,0:T(8,128)(2,1)} %broadcast_select_fusion), calls=%async_computation | async-start | bytes 6291456 | tf_op jit(solution)/shard_map/all_to_all | solution.py:133

commit v2 on v1

v2 whole, which is shorter than its diff:
```python
import functools

import jax
import jax.numpy as jnp
from jax import lax
from jax.experimental import pallas as pl
from jax.experimental.pallas import tpu as pltpu
from jax.sharding import PartitionSpec as P

BLOCK = 256


def shifted(block, axis, distance):
    devices = range(lax.axis_size(axis))
    route = [(i - distance, i) for i in devices if i - distance in devices]
    return lax.ppermute(block, axis, route)


def compact_kernel(nb_ref, list_ref, pos_ref, *, absent):
    offsets, block = nb_ref.shape
    value = nb_ref[...]
    present = value != absent
    lane = lax.broadcasted_iota(jnp.int32, (offsets, block), 1)
    before = lax.broadcasted_iota(jnp.int32, (block, block), 0)
    after = lax.broadcasted_iota(jnp.int32, (block, block), 1)
    triangle = jnp.where(before <= after, 1.0, 0.0).astype(jnp.bfloat16)
    ones = jnp.where(present, 1.0, 0.0).astype(jnp.bfloat16)
    counted = jnp.dot(ones, triangle, preferred_element_type=jnp.float32).astype(jnp.int32)
    pos = counted - 1
    pos_ref[...] = jnp.where(present, pos, -1)
    word = jnp.where(present, value + (lane - pos) * 16384 + (1 << 23), 0)
    for bit in range(block.bit_length() - 1):
        moves = (word & (16384 << bit)) != 0
        moved = pltpu.roll(jnp.where(moves, word, 0), block - (1 << bit), 1)
        word = jnp.where(moves, 0, word) + moved
    list_ref[...] = jnp.where(word != 0, word & 16383, absent)


def conv_kernel(
    list_ref,
    pos_ref,
    feat_ref,
    low_ref,
    up_ref,
    w_ref,
    gain_ref,
    shift_ref,
    out_ref,
    tab_ref,
    buf_a,
    buf_b,
    acc_ref,
):
    step = pl.program_id(0)
    rows, channels = feat_ref.shape
    halo = low_ref.shape[0]
    offsets, block = list_ref.shape
    half = block // 2
    middle = offsets // 2
    absent = rows + 2 * halo
    table = tab_ref.reshape(tab_ref.shape[0], 1, channels)
    slots = lax.broadcasted_iota(jnp.int32, (half, block), 0)

    @pl.when(step == 0)
    def _():
        chunk = 256
        for src, start in ((feat_ref, 0), (low_ref, rows), (up_ref, rows + halo)):

            @pl.loop(0, src.shape[0] // chunk)
            def _(i, src=src, start=start):
                at = pl.multiple_of(i * chunk, chunk)
                tab_ref[pl.ds(start + at, chunk), :] = src[pl.ds(at, chunk), :].astype(jnp.float32)

        tab_ref[pl.ds(absent, 8), :] = jnp.zeros((8, channels), jnp.float32)

    def offset_of(pair, j):
        at = 2 * pair + j
        return at + jnp.where(at >= middle, 1, 0)

    def gather(pair, buf, base=0):
        for j in range(2):
            k = offset_of(pair, j)
            for c in range(half):
                buf[pl.ds(j * half + c, 1), :] = table[list_ref[k, base + c]]

    def multiply(pair, buf, base=0):
        products, spreads = [], []
        for j in range(2):
            k = offset_of(pair, j)
            rows_in = buf[j * half : (j + 1) * half, :].astype(jnp.bfloat16)
            products.append(
                lax.dot_general(
                    w_ref[k], rows_in, (((1,), (1,)), ((), ())), preferred_element_type=jnp.float32
                )
            )
            wanted = pos_ref[pl.ds(k, 1), :] - base
            spreads.append(jnp.where(slots == wanted, 1.0, 0.0).astype(jnp.bfloat16))
        product = jnp.concatenate(products, axis=1)
        high = product.astype(jnp.bfloat16)
        low = (product - high.astype(jnp.float32)).astype(jnp.bfloat16)
        both = jnp.concatenate([high, low], axis=0)
        spread = jnp.concatenate(spreads, axis=0)
        result = jnp.dot(both, spread, preferred_element_type=jnp.float32)
        acc_ref[...] += result[:channels] + result[channels:]

    own = feat_ref[pl.ds(pl.multiple_of(step * block, block), block), :]
    gather(0, buf_a)
    acc_ref[...] = lax.dot_general(
        w_ref[middle], own, (((1,), (1,)), ((), ())), preferred_element_type=jnp.float32
    )

    pairs = middle

    @pl.loop(0, pairs // 2)
    def _(p):
        first = 2 * p
        gather(first + 1, buf_b)
        multiply(first, buf_a)
        gather(first + 2, buf_a)
        multiply(first + 1, buf_b)

    multiply(pairs - 1, buf_a)

    crowded = jnp.int32(0)
    for k in range(offsets):
        if k != middle:
            crowded = crowded + jnp.where(list_ref[k, half] != absent, 1, 0)

    @pl.when(crowded > 0)
    def _():

        @pl.loop(0, pairs)
        def _(p):
            more = (list_ref[offset_of(p, 0), half] != absent) | (
                list_ref[offset_of(p, 1), half] != absent
            )

            @pl.when(more)
            def _():
                gather(p, buf_a, half)
                multiply(p, buf_a, half)

    summed = acc_ref[...].T
    centered = summed - jnp.mean(summed, axis=-1, keepdims=True)
    spread_sq = jnp.mean(centered * centered, axis=-1, keepdims=True)
    normed = centered * lax.rsqrt(spread_sq + 1e-05) * gain_ref[...] + shift_ref[...]
    blended = own.astype(jnp.float32) + normed / (1.0 + jnp.exp(-normed))
    out_ref[...] = blended.astype(jnp.bfloat16)


def compact(columns, absent):
    offsets, rows = columns.shape
    spec = pl.BlockSpec((offsets, BLOCK), lambda i: (0, i))
    shape = jax.ShapeDtypeStruct((offsets, rows), jnp.int32)
    return pl.pallas_call(
        functools.partial(compact_kernel, absent=absent),
        grid=(rows // BLOCK,),
        out_shape=(shape, shape),
        in_specs=[spec],
        out_specs=(spec, spec),
        cost_estimate=pl.CostEstimate(
            flops=100 * rows * offsets, bytes_accessed=12 * rows * offsets, transcendentals=0
        ),
    )(columns)


def conv_block(features, from_lower, from_upper, lists, places, weights, gain, shift):
    rows, channels = features.shape
    halo = from_lower.shape[0]
    offsets = lists.shape[0]
    block = BLOCK
    whole = pl.BlockSpec(memory_space=pltpu.VMEM)
    return pl.pallas_call(
        conv_kernel,
        grid=(rows // block,),
        out_shape=jax.ShapeDtypeStruct((rows, channels), jnp.bfloat16),
        in_specs=[
            pl.BlockSpec((offsets, block), lambda i: (0, i), memory_space=pltpu.SMEM),
            pl.BlockSpec((offsets, block), lambda i: (0, i)),
            whole,
            whole,
            whole,
            whole,
            whole,
            whole,
        ],
        out_specs=pl.BlockSpec((block, channels), lambda i: (i, 0)),
        scratch_shapes=[
            pltpu.VMEM((rows + 2 * halo + 8, channels), jnp.float32),
            pltpu.VMEM((block, channels), jnp.float32),
            pltpu.VMEM((block, channels), jnp.float32),
            pltpu.VMEM((channels, block), jnp.float32),
        ],
        compiler_params=pltpu.CompilerParams(vmem_limit_bytes=48 * 1024 * 1024),
        cost_estimate=pl.CostEstimate(
            flops=2 * rows * offsets * channels * channels,
            bytes_accessed=8 * rows * channels,
            transcendentals=rows * channels,
        ),
    )(lists, places, features, from_lower, from_upper, weights, gain, shift)


def body(
    features, neighbors, send_low, send_high, send_slot, recv_slot, kernel, norm_gain, norm_shift
):
    row_count, channels = features.shape
    zero_row = jnp.zeros((1, channels), jnp.bfloat16)
    weights = lax.all_gather(kernel.transpose(0, 2, 1), "grp", axis=1, tiled=True)
    upward = jnp.take(features, send_high, axis=0)
    downward = jnp.take(features, send_low, axis=0)
    from_lower = shifted(upward, "brick", 1)
    from_upper = shifted(downward, "brick", -1)
    lists, places = compact(neighbors.T, row_count + 2 * send_low.shape[0])
    blended = conv_block(
        features,
        from_lower,
        from_upper,
        lists,
        places,
        weights,
        norm_gain.reshape(1, channels),
        norm_shift.reshape(1, channels),
    )
    slab_count = lax.axis_size("brick")
    capacity = send_slot.shape[0] // slab_count
    padded = jnp.concatenate([blended, zero_row], axis=0)
    outbox = jnp.take(padded, send_slot, axis=0)
    arrived = lax.all_to_all(
        outbox.reshape(slab_count, capacity, channels),
        "brick",
        split_axis=0,
        concat_axis=0,
        tiled=True,
    )
    return jnp.take(arrived.reshape(slab_count * capacity, channels), recv_slot, axis=0)


def solution(mesh):
    return jax.shard_map(
        body,
        mesh=mesh,
        in_specs=(
            P(("brick", "grp"), None),
            P(("brick", "grp"), None),
            P(("brick", "grp")),
            P(("brick", "grp")),
            P(("brick", "grp")),
            P(("brick", "grp")),
            P(None, None, "grp"),
            P(),
            P(),
        ),
        out_specs=P(("brick", "grp"), None),
        check_vma=False,
    )
```

time: 445 us -> 409 us (0.919)
  Pallas kernels: 268 us -> 229 us
    pallas_call x1, Pallas kernels: 268 us -> 204 us  [conv_block(): pl.pallas_call(conv_kernel, grid=(rows // block,), out_shape=jax.ShapeDty...]
    pallas_call x0 -> x1, Pallas kernels: none -> 25 us  [compact(): pl.pallas_call(functools.partial(compact_kernel, absent=absent), grid=(ro...]
  transfers between devices with their start and end apart: 3 -> 3, of which waited for: 1 -> 1; matrix products, arithmetic and copies ran while one was open for 2% -> 2% of each run, Pallas kernels for 0% -> 6%
where the time goes in v2:
time: 409 us; the launch traced here: 401 us
  Pallas kernels  229 us (56%)
  local copies, waits for them, and re-layouts  89.3 us (22%)
  waiting for transfers between devices  34.4 us (8%)
  blocking collectives  18.9 us (5%)
  other arithmetic  16.7 us (4%)
  starting transfers between devices  13 us (3%)
    pallas_call x1, Pallas kernels, conv_block(): pl.pallas_call(conv_kernel, grid=(rows // block,), out_shape=jax.ShapeDty...  204 us
    gather x1, local copies, waits for them, and re-layouts, body(): outbox = jnp.take(padded, send_slot, axis=0)  43.3 us
    all_to_all x1, waiting for transfers between devices, body(): lax.all_to_all(outbox.reshape(slab_count, capacity, channels), 'brick', s...  34.4 us
    gather x1, local copies, waits for them, and re-layouts, body(): jnp.take(arrived.reshape(slab_count * capacity, channels), recv_slot, axi...  29.5 us
    pallas_call x1, Pallas kernels, compact(): pl.pallas_call(functools.partial(compact_kernel, absent=absent), grid=(ro...  25 us
    all_gather x1, blocking collectives, body(): lax.all_gather(kernel.transpose(0, 2, 1), 'grp', axis=1, tiled=True)  18.9 us
  transfers between devices with their start and end apart: 3, of which 1 were waited for; matrix products, arithmetic and copies ran while one was open for 2% of the time, Pallas kernels for 6%

profile of v2, /device:TPU:1, one launch (start us, length us, event | category | flops | bytes accessed | tf_op | source)
XLA Modules:
  0.0 401.5 jit_solution(5888599736570196154)
XLA Ops:
  0.0 0.7 fusion.2
  0.7 0.7 compare_and_fusion.3
  1.4 0.0 copy-start.8
  1.4 0.0 copy-start.4
  1.4 7.6 %gather_fusion.2 = bf16[2048,128]{1,0:T(8,128)(2,1)S(1)} fusion(bf16[8192,128]{1,0:T(8,128)(2,1)} %feat_ref.1, s32[2048]{0:T(1024)S(1)} %fusion.2), kind=kCustom, calls=%fused_computation.clone | custom fusion | bytes 1056768 | tf_op jit(solution)/shard_map/jit(_take)/gather | solution.py:209
  9.0 1.2 broadcast_select_fusion.3
  10.2 4.5 %collective-permute-start = (bf16[2048,128]{1,0:T(8,128)(2,1)}, bf16[2048,128]{1,0:T(8,128)(2,1)S(1)}, u32[]{:S(2)}, u32[]{:S(2)}) collective-permute-start(bf16[2048,128]{1,0:T(8,128)(2,1)} %broadcast_select_fusion.3), channel_id=1, source_target_pairs={{0,4},{4,8},{8,12},{12,16},{16,20},{20,24},{24,28},{1,5},{5,9},{9,... | collective-permute-start | bytes 1572872 | tf_op jit(solution)/shard_map/ppermute | solution.py:16
  14.7 0.0 copy-done.8
  14.7 0.0 copy-done.4
  14.8 0.0 copy-start.6
  14.8 0.0 copy-start.5
  14.8 6.2 %gather_fusion.3 = bf16[2048,128]{1,0:T(8,128)(2,1)S(1)} fusion(bf16[8192,128]{1,0:T(8,128)(2,1)S(1)} %copy-done.4, s32[2048]{0:T(1024)S(1)} %fusion.3), kind=kCustom, calls=%fused_computation.1.clone | custom fusion | bytes 1056768 | tf_op jit(solution)/shard_map/jit(_take)/gather | solution.py:210
  21.0 0.0 copy-start.2
  21.0 0.0 copy-start.3
  21.0 0.3 broadcast_select_fusion.2
  21.3 1.9 collective-permute-start.1
  23.3 0.0 copy-done.6
  23.3 0.0 copy-done.5
  23.3 18.9 %all_gather.3.w_ref = bf16[27,128,128]{2,1,0:T(8,128)(2,1)S(1)} all-gather(bf16[27,32,128]{2,1,0:T(8,128)(2,1)S(1)} %bitcast.11), channel_id=1, replica_groups=mesh['brick'=8,'grp'=4] {'grp'}, dimensions={1}, use_global_device_ids=true | all-gather | bytes 1105920 | tf_op jit(solution)/shard_map/all_gather | solution.py:208
  42.2 0.1 broadcast_in_dim.37
  42.2 25.0 %shard_map.91 = (s32[27,8192]{1,0:T(8,128)}, s32[27,8192]{1,0:T(8,128)}) custom-call(s32[27,8192]{1,0:T(8,128)} %bitcast.10), custom_call_target="tpu_custom_call" | custom-call | flops 22118400 | bytes 2654208 | tf_op jit(solution)/shard_map/pallas_call | solution.py:155
  67.3 0.0 collective-permute-done.low_ref
  67.3 0.0 collective-permute-done.1.up_ref
  67.3 0.0 copy-done.2
  67.3 0.0 copy-done.3
  67.3 0.0 copy-start
  67.3 1.2 copy-done
  68.6 0.0 copy-start.1
  68.6 1.2 copy-done.1
  69.8 203.9 %shard_map.92 = bf16[8192,128]{1,0:T(8,128)(2,1)S(1)} custom-call(s32[27,8192]{1,0:T(8,128)S(1)} %copy-done, s32[27,8192]{1,0:T(8,128)S(1)} %copy-done.1, bf16[8192,128]{1,0:T(8,128)(2,1)} %feat_ref.1, bf16[2048,128]{1,0:T(8,128)(2,1)S(1)} %collective-permute-done.low_ref, bf16[2048,128]{1,0:T(8,128)(2,1)S(1)} %collective-permute-done.1.up_ref, ...), custom_call_target="tpu_custom_call" | custom-call | flops 7247757312 | bytes 8388608 | tf_op jit(solution)/shard_map/pallas_call | solution.py:173
  273.7 0.2 concatenate.3
  273.9 43.3 %gather_fusion = bf16[12288,128]{1,0:T(8,128)(2,1)} fusion(bf16[8193,128]{1,0:T(8,128)(2,1)S(1)} %concatenate.3, s32[12288]{0:T(1024)S(1)} %fusion), kind=kCustom, calls=%fused_computation.2 | custom fusion | bytes 6340608 | tf_op jit(solution)/shard_map/jit(_take)/gather | solution.py:227
  317.2 7.2 %broadcast_select_fusion = bf16[8,1536,128]{2,1,0:T(8,128)(2,1)} fusion(bf16[8,1536,128]{2,1,0:T(8,128)(2,1)} %bitcast.9, pred[8,1536]{1,0:T(8,128)(4,1)S(1)} %broadcast_in_dim.37), kind=kLoop, calls=%fused_computation.4 | loop fusion | flops 1572864 | bytes 6303744 | tf_op jit(solution)/shard_map/jit(_take)/select_n | solution.py:227
  324.4 0.0 copy-start.7
  324.4 6.6 %all-to-all-start = ((bf16[8,1536,128]{2,1,0:T(8,128)(2,1)}), bf16[8,1536,128]{2,1,0:T(8,128)(2,1)S(1)}, u32[]{:S(2)}, u32[]{:S(2)}) async-start(bf16[8,1536,128]{2,1,0:T(8,128)(2,1)} %broadcast_select_fusion), calls=%async_computation | async-start | bytes 6291456 | tf_op jit(solution)/shard_map/all_to_all | solution.py:228
  331.0 0.0 copy-done.7
  331.1 34.4 %all-to-all-done = bf16[8,1536,128]{2,1,0:T(8,128)(2,1)S(1)} async-done(((bf16[8,1536,128]{2,1,0:T(8,128)(2,1)}), bf16[8,1536,128]{2,1,0:T(8,128)(2,1)S(1)}, u32[]{:S(2)}, u32[]{:S(2)}) %all-to-all-start) | async-done | bytes 3145760 | tf_op jit(solution)/shard_map/all_to_all | solution.py:228
  365.5 29.5 %gather_fusion.1 = bf16[8192,128]{1,0:T(8,128)(2,1)} fusion(bf16[12288,128]{1,0:T(8,128)(2,1)S(1)} %bitcast.8, s32[8192]{0:T(1024)S(1)} %fusion.1), kind=kCustom, calls=%fused_computation.3 | custom fusion | bytes 4227072 | tf_op jit(solution)/shard_map/jit(_take)/gather | solution.py:235
  394.9 6.6 %broadcast_select_fusion.1 = bf16[8192,128]{1,0:T(8,128)(2,1)} fusion(bf16[8192,128]{1,0:T(8,128)(2,1)} %gather_fusion.1, pred[8192]{0:T(1024)(128)(4,1)S(1)} %compare_and_fusion.1), kind=kLoop, calls=%fused_computation.5 | loop fusion | flops 1048576 | bytes 4202496 | tf_op jit(solution)/shard_map/jit(_take)/select_n | solution.py:235
  (6 shorter events, 0.1 us)
Async XLA Ops:
  1.4 13.3 %copy-start.8 = (s32[2048]{0:T(1024)S(1)}, s32[2048]{0:T(1024)}, u32[]{:S(2)}) copy-start(s32[2048]{0:T(1024)} %param.13) | copy-start | bytes 24580
  1.4 13.3 %copy-start.4 = (bf16[8192,128]{1,0:T(8,128)(2,1)S(1)}, bf16[8192,128]{1,0:T(8,128)(2,1)}, u32[]{:S(2)}) copy-start(bf16[8192,128]{1,0:T(8,128)(2,1)} %feat_ref.1) | copy-start | bytes 6291460
  10.2 57.1 %collective-permute-start = (bf16[2048,128]{1,0:T(8,128)(2,1)}, bf16[2048,128]{1,0:T(8,128)(2,1)S(1)}, u32[]{:S(2)}, u32[]{:S(2)}) collective-permute-start(bf16[2048,128]{1,0:T(8,128)(2,1)} %broadcast_select_fusion.3), channel_id=1, source_target_pairs={{0,4},{4,8},{8,12},{12,16},{16,20},{20,24},{24,28},{1,5},{5,9},{9,... | collective-permute-start | bytes 1572872 | tf_op jit(solution)/shard_map/ppermute | solution.py:16
  14.8 8.5 %copy-start.6 = (s32[12288]{0:T(1024)S(1)}, s32[12288]{0:T(1024)}, u32[]{:S(2)}) copy-start(s32[12288]{0:T(1024)} %param.15) | copy-start | bytes 147460
  14.8 8.5 %copy-start.5 = (bf16[27,128,32]{1,2,0:T(8,128)(2,1)S(1)}, bf16[27,128,32]{1,2,0:T(8,128)(2,1)}, u32[]{:S(2)}) copy-start(bf16[27,128,32]{1,2,0:T(8,128)(2,1)} %param.17) | copy-start | bytes 663556
  21.0 46.3 %copy-start.2 = (f32[128]{0:T(128)S(1)}, f32[128]{0:T(128)}, u32[]{:S(2)}) copy-start(f32[128]{0:T(128)} %param.18) | copy-start | bytes 1540
  21.0 46.3 %copy-start.3 = (f32[128]{0:T(128)S(1)}, f32[128]{0:T(128)}, u32[]{:S(2)}) copy-start(f32[128]{0:T(128)} %param.19) | copy-start | bytes 1540
  21.3 46.0 %collective-permute-start.1 = (bf16[2048,128]{1,0:T(8,128)(2,1)S(1)}, bf16[2048,128]{1,0:T(8,128)(2,1)S(1)}, u32[]{:S(2)}, u32[]{:S(2)}) collective-permute-start(bf16[2048,128]{1,0:T(8,128)(2,1)S(1)} %broadcast_select_fusion.2), channel_id=1, source_target_pairs={{4,0},{8,4},{12,8},{16,12},{20,16},{24,20},{28,24},{5,1},{9,5},{13... | collective-permute-start | bytes 1572872 | tf_op jit(solution)/shard_map/ppermute | solution.py:16
  67.3 1.2 copy-start
  68.6 1.2 copy-start.1
  324.4 6.6 %copy-start.7 = (s32[8192]{0:T(1024)S(1)}, s32[8192]{0:T(1024)}, u32[]{:S(2)}) copy-start(s32[8192]{0:T(1024)} %param.16) | copy-start | bytes 98308
  324.4 41.0 %all-to-all-start = ((bf16[8,1536,128]{2,1,0:T(8,128)(2,1)}), bf16[8,1536,128]{2,1,0:T(8,128)(2,1)S(1)}, u32[]{:S(2)}, u32[]{:S(2)}) async-start(bf16[8,1536,128]{2,1,0:T(8,128)(2,1)} %broadcast_select_fusion), calls=%async_computation | async-start | bytes 6291456 | tf_op jit(solution)/shard_map/all_to_all | solution.py:228

commit v3 on v2

--- a/solution.py
+++ b/solution.py
@@ -200,11 +200,144 @@
     )(lists, places, features, from_lower, from_upper, weights, gain, shift)
 
 
+def relay_kernel(
+    send_ref,
+    recv_ref,
+    rows_ref,
+    out_ref,
+    table_ref,
+    stage_ref,
+    outbox_ref,
+    inbox_ref,
+    arrived_ref,
+    send_sem,
+    recv_sem,
+    *,
+    axis,
+    count,
+):
+    me = lax.axis_index(axis)
+    rows, channels = rows_ref.shape
+    capacity = outbox_ref.shape[1]
+    chunk = stage_ref.shape[0]
+    table = table_ref.reshape(table_ref.shape[0], 1, channels)
+    arrived = arrived_ref.reshape(arrived_ref.shape[0], 1, channels)
+
+    barrier = pltpu.get_barrier_semaphore()
+
+    @pl.loop(1, count)
+    def _(j):
+        pl.semaphore_signal(
+            barrier,
+            inc=1,
+            device_id={axis: lax.rem(me + j, count)},
+            device_id_type=pl.DeviceIdType.MESH,
+        )
+
+    @pl.loop(0, rows // chunk)
+    def _(i):
+        at = pl.ds(pl.multiple_of(i * chunk, chunk), chunk)
+        table_ref[at, :] = rows_ref[at, :].astype(jnp.float32)
+
+    table_ref[pl.ds(rows, 8), :] = jnp.zeros((8, channels), jnp.float32)
+    pl.semaphore_wait(barrier, count - 1)
+
+    def copy_to(j):
+        to = lax.rem(me + j, count)
+        return pltpu.make_async_remote_copy(
+            src_ref=outbox_ref.at[to],
+            dst_ref=inbox_ref.at[me],
+            send_sem=send_sem.at[j],
+            recv_sem=recv_sem.at[j],
+            device_id={axis: to},
+            device_id_type=pl.DeviceIdType.MESH,
+        )
+
+    def fill(shard, into_ref):
+        @pl.loop(0, capacity // chunk)
+        def _(i):
+            first = pl.multiple_of(i * chunk, chunk)
+            for c in range(chunk):
+                stage_ref[pl.ds(c, 1), :] = table[send_ref[shard * capacity + first + c]]
+            into_ref[pl.ds(first, chunk), :] = stage_ref[...].astype(jnp.bfloat16)
+
+    @pl.loop(0, count - 1)
+    def _(i):
+        j = lax.rem(i + count // 2, count - 1) + 1
+        fill(lax.rem(me + j, count), outbox_ref.at[lax.rem(me + j, count)])
+        copy_to(j).start()
+
+    fill(me, inbox_ref.at[me])
+
+    def widen(source):
+        @pl.loop(0, capacity // chunk)
+        def _(i):
+            first = pl.multiple_of(i * chunk, chunk)
+            to = pl.multiple_of(source * capacity + first, chunk)
+            arrived_ref[pl.ds(to, chunk), :] = inbox_ref[source, pl.ds(first, chunk), :].astype(
+                jnp.float32
+            )
+
+    widen(me)
+
+    @pl.loop(0, count - 1)
+    def _(i):
+        j = lax.rem(i + count // 2, count - 1) + 1
+        source = lax.rem(me - j + count, count)
+        pltpu.make_async_remote_copy(
+            src_ref=outbox_ref.at[source],
+            dst_ref=inbox_ref.at[source],
+            send_sem=send_sem.at[j],
+            recv_sem=recv_sem.at[j],
+            device_id={axis: source},
+            device_id_type=pl.DeviceIdType.MESH,
+        ).wait_recv()
+        widen(source)
+
+    @pl.loop(0, rows // chunk)
+    def _(i):
+        first = pl.multiple_of(i * chunk, chunk)
+        for c in range(chunk):
+            stage_ref[pl.ds(c, 1), :] = arrived[recv_ref[first + c]]
+        out_ref[pl.ds(first, chunk), :] = stage_ref[...].astype(jnp.bfloat16)
+
+    @pl.loop(1, count)
+    def _(j):
+        copy_to(j).wait_send()
+
+
+def relay(blended, send_slot, recv_slot, axis):
+    rows, channels = blended.shape
+    count = lax.axis_size(axis)
+    capacity = send_slot.shape[0] // count
+    chunk = 128
+    whole = pl.BlockSpec(memory_space=pltpu.VMEM)
+    scalars = pl.BlockSpec(memory_space=pltpu.SMEM)
+    boxes = pltpu.VMEM((count, capacity, channels), jnp.bfloat16)
+    return pl.pallas_call(
+        functools.partial(relay_kernel, axis=axis, count=count),
+        out_shape=jax.ShapeDtypeStruct((rows, channels), jnp.bfloat16),
+        in_specs=[scalars, scalars, whole],
+        out_specs=whole,
+        scratch_shapes=[
+            pltpu.VMEM((rows + 8, channels), jnp.float32),
+            pltpu.VMEM((chunk, channels), jnp.float32),
+            boxes,
+            boxes,
+            pltpu.VMEM((count * capacity, channels), jnp.float32),
+            pltpu.SemaphoreType.DMA((count,)),
+            pltpu.SemaphoreType.DMA((count,)),
+        ],
+        compiler_params=pltpu.CompilerParams(
+            collective_id=0, has_side_effects=True, vmem_limit_bytes=48 * 1024 * 1024
+        ),
+    )(send_slot, recv_slot, blended)
+
+
 def body(
     features, neighbors, send_low, send_high, send_slot, recv_slot, kernel, norm_gain, norm_shift
 ):
     row_count, channels = features.shape
-    zero_row = jnp.zeros((1, channels), jnp.bfloat16)
     weights = lax.all_gather(kernel.transpose(0, 2, 1), "grp", axis=1, tiled=True)
     upward = jnp.take(features, send_high, axis=0)
     downward = jnp.take(features, send_low, axis=0)
@@ -221,18 +354,7 @@
         norm_gain.reshape(1, channels),
         norm_shift.reshape(1, channels),
     )
-    slab_count = lax.axis_size("brick")
-    capacity = send_slot.shape[0] // slab_count
-    padded = jnp.concatenate([blended, zero_row], axis=0)
-    outbox = jnp.take(padded, send_slot, axis=0)
-    arrived = lax.all_to_all(
-        outbox.reshape(slab_count, capacity, channels),
-        "brick",
-        split_axis=0,
-        concat_axis=0,
-        tiled=True,
-    )
-    return jnp.take(arrived.reshape(slab_count * capacity, channels), recv_slot, axis=0)
+    return relay(blended, send_slot, recv_slot, "brick")
 
 
 def solution(mesh):

time: 409 us -> 332 us (0.81); the launches traced: 401 us -> 329 us
  local copies, waits for them, and re-layouts: 89.3 us -> 17.6 us
  Pallas kernels: 229 us -> 283 us
  waiting for transfers between devices: 34.4 us -> 0.01 us
  other arithmetic: 16.7 us -> 2.92 us
  starting transfers between devices: 13 us -> 6.42 us
    gather x2 -> x0, local copies, waits for them, and re-layouts: 72.8 us -> none  [the longest x1 43.3 us: body(): outbox = jnp.take(padded, send_slot, axis=0)]
    pallas_call x0 -> x1, Pallas kernels: none -> 53.8 us  [relay(): pl.pallas_call(functools.partial(relay_kernel, axis=axis, count=count), o...]
    all_to_all x1 -> x0, waiting for transfers between devices: 34.4 us -> none  [body(): lax.all_to_all(outbox.reshape(slab_count, capacity, channels), 'brick', s...]
    select_n x2 -> x0, other arithmetic: 13.7 us -> none  [the longest x1 7.17 us: body(): outbox = jnp.take(padded, send_slot, axis=0)]
    all_to_all x1 -> x0, starting transfers between devices: 6.62 us -> none  [body(): lax.all_to_all(outbox.reshape(slab_count, capacity, channels), 'brick', s...]
  transfers between devices with their start and end apart: 3 -> 2, of which waited for: 1 -> 0; matrix products, arithmetic and copies ran while one was open for 2% -> 2% of each run, Pallas kernels for 6% -> 8%
where the time goes in v3:
time: 332 us; the launch traced here: 329 us
  Pallas kernels  283 us (85%)
  blocking collectives  19 us (6%)
  local copies, waits for them, and re-layouts  17.6 us (5%)
  starting transfers between devices  6.42 us (2%)
    pallas_call x1, Pallas kernels, conv_block(): pl.pallas_call(conv_kernel, grid=(rows // block,), out_shape=jax.ShapeDty...  204 us
    pallas_call x1, Pallas kernels, relay(): pl.pallas_call(functools.partial(relay_kernel, axis=axis, count=count), o...  53.8 us
    pallas_call x1, Pallas kernels, compact(): pl.pallas_call(functools.partial(compact_kernel, absent=absent), grid=(ro...  25 us
    all_gather x1, blocking collectives, body(): lax.all_gather(kernel.transpose(0, 2, 1), 'grp', axis=1, tiled=True)  19 us
    gather x1, local copies, waits for them, and re-layouts, body(): downward = jnp.take(features, send_low, axis=0)  7.61 us
  transfers between devices with their start and end apart: 2, of which 0 were waited for; matrix products, arithmetic and copies ran while one was open for 2% of the time, Pallas kernels for 8%

profile of v3, /device:TPU:1, one launch (start us, length us, event | category | flops | bytes accessed | tf_op | source)
XLA Modules:
  0.0 328.6 jit_solution(12029420369899860039)
XLA Ops:
  0.0 0.7 compare_and_fusion
  0.7 0.7 fusion.1
  1.4 0.0 copy-start.8
  1.4 0.0 copy-start.6
  1.4 7.6 %gather_fusion.1 = bf16[2048,128]{1,0:T(8,128)(2,1)S(1)} fusion(bf16[8192,128]{1,0:T(8,128)(2,1)} %feat_ref.1, s32[2048]{0:T(1024)S(1)} %fusion.1), kind=kCustom, calls=%fused_computation.1.clone | custom fusion | bytes 1056768 | tf_op jit(solution)/shard_map/jit(_take)/gather | solution.py:343
  9.0 1.2 broadcast_select_fusion
  10.2 1.9 collective-permute-start.1
  12.1 0.0 copy-done.8
  12.2 0.0 copy-done.6
  12.2 6.2 %gather_fusion = bf16[2048,128]{1,0:T(8,128)(2,1)S(1)} fusion(bf16[8192,128]{1,0:T(8,128)(2,1)S(1)} %copy-done.6, s32[2048]{0:T(1024)S(1)} %fusion), kind=kCustom, calls=%fused_computation.clone | custom fusion | bytes 1056768 | tf_op jit(solution)/shard_map/jit(_take)/gather | solution.py:342
  18.4 0.0 copy-start.7
  18.4 0.0 copy-start.4
  18.4 0.0 copy-start.5
  18.4 0.3 broadcast_select_fusion.1
  18.8 4.5 %collective-permute-start = (bf16[2048,128]{1,0:T(8,128)(2,1)S(1)}, bf16[2048,128]{1,0:T(8,128)(2,1)S(1)}, u32[]{:S(2)}, u32[]{:S(2)}) collective-permute-start(bf16[2048,128]{1,0:T(8,128)(2,1)S(1)} %broadcast_select_fusion.1), channel_id=1, source_target_pairs={{0,4},{4,8},{8,12},{12,16},{16,20},{20,24},{24,28},{1,5},{5,9},{9,... | collective-permute-start | bytes 1572872 | tf_op jit(solution)/shard_map/ppermute | solution.py:16
  23.2 25.0 %shard_map.91 = (s32[27,8192]{1,0:T(8,128)}, s32[27,8192]{1,0:T(8,128)}) custom-call(s32[27,8192]{1,0:T(8,128)} %bitcast.6), custom_call_target="tpu_custom_call" | custom-call | flops 22118400 | bytes 2654208 | tf_op jit(solution)/shard_map/pallas_call | solution.py:155
  48.3 0.0 copy-done.7
  48.3 19.0 %all_gather.3.w_ref = bf16[27,128,128]{2,1,0:T(8,128)(2,1)S(1)} all-gather(bf16[27,32,128]{2,1,0:T(8,128)(2,1)S(1)} %bitcast.7), channel_id=1, replica_groups=mesh['brick'=8,'grp'=4] {'grp'}, dimensions={1}, use_global_device_ids=true | all-gather | bytes 1105920 | tf_op jit(solution)/shard_map/all_gather | solution.py:341
  67.3 0.0 collective-permute-done.1.up_ref
  67.3 0.0 collective-permute-done.low_ref
  67.3 0.0 copy-done.4
  67.3 0.0 copy-done.5
  67.3 0.0 copy-start.2
  67.3 1.2 copy-done.2
  68.5 0.0 copy-start.3
  68.5 1.2 copy-done.3
  69.7 0.0 copy-start
  69.7 0.0 copy-start.1
  69.7 203.8 %shard_map.92.rows_ref = bf16[8192,128]{1,0:T(8,128)(2,1)S(1)} custom-call(s32[27,8192]{1,0:T(8,128)S(1)} %copy-done.2, s32[27,8192]{1,0:T(8,128)S(1)} %copy-done.3, bf16[8192,128]{1,0:T(8,128)(2,1)} %feat_ref.1, bf16[2048,128]{1,0:T(8,128)(2,1)S(1)} %collective-permute-done.low_ref, bf16[2048,128]{1,0:T(8,128)(2,1)S(1)} %collective-permute-done.1.up_ref, ...), custom_call_target="tpu_custom_call" | custom-call | flops 7247757312 | bytes 8388608 | tf_op jit(solution)/shard_map/pallas_call | solution.py:173
  273.5 0.0 copy-done
  273.5 0.0 copy-done.1
  273.5 53.8 %shard_map.93 = bf16[8192,128]{1,0:T(8,128)(2,1)S(1)} custom-call(s32[12288]{0:T(1024)S(1)} %copy-done, s32[8192]{0:T(1024)S(1)} %copy-done.1, bf16[8192,128]{1,0:T(8,128)(2,1)S(1)} %shard_map.92.rows_ref), custom_call_target="tpu_custom_call" | custom-call | tf_op jit(solution)/shard_map/pallas_call | solution.py:317
  327.3 1.3 copy.11
  (2 shorter events, 0.0 us)
Async XLA Ops:
  1.4 10.7 %copy-start.8 = (s32[2048]{0:T(1024)S(1)}, s32[2048]{0:T(1024)}, u32[]{:S(2)}) copy-start(s32[2048]{0:T(1024)} %param.14) | copy-start | bytes 24580
  1.4 10.8 %copy-start.6 = (bf16[8192,128]{1,0:T(8,128)(2,1)S(1)}, bf16[8192,128]{1,0:T(8,128)(2,1)}, u32[]{:S(2)}) copy-start(bf16[8192,128]{1,0:T(8,128)(2,1)} %feat_ref.1) | copy-start | bytes 6291460
  10.2 57.1 %collective-permute-start.1 = (bf16[2048,128]{1,0:T(8,128)(2,1)}, bf16[2048,128]{1,0:T(8,128)(2,1)S(1)}, u32[]{:S(2)}, u32[]{:S(2)}) collective-permute-start(bf16[2048,128]{1,0:T(8,128)(2,1)} %broadcast_select_fusion), channel_id=1, source_target_pairs={{4,0},{8,4},{12,8},{16,12},{20,16},{24,20},{28,24},{5,1},{9,5},{13... | collective-permute-start | bytes 1572872 | tf_op jit(solution)/shard_map/ppermute | solution.py:16
  18.4 29.9 %copy-start.7 = (bf16[27,128,32]{1,2,0:T(8,128)(2,1)S(1)}, bf16[27,128,32]{1,2,0:T(8,128)(2,1)}, u32[]{:S(2)}) copy-start(bf16[27,128,32]{1,2,0:T(8,128)(2,1)} %param.17) | copy-start | bytes 663556
  18.4 48.9 %copy-start.4 = (f32[128]{0:T(128)S(1)}, f32[128]{0:T(128)}, u32[]{:S(2)}) copy-start(f32[128]{0:T(128)} %param.18) | copy-start | bytes 1540
  18.4 48.9 %copy-start.5 = (f32[128]{0:T(128)S(1)}, f32[128]{0:T(128)}, u32[]{:S(2)}) copy-start(f32[128]{0:T(128)} %param.19) | copy-start | bytes 1540
  18.8 48.5 %collective-permute-start = (bf16[2048,128]{1,0:T(8,128)(2,1)S(1)}, bf16[2048,128]{1,0:T(8,128)(2,1)S(1)}, u32[]{:S(2)}, u32[]{:S(2)}) collective-permute-start(bf16[2048,128]{1,0:T(8,128)(2,1)S(1)} %broadcast_select_fusion.1), channel_id=1, source_target_pairs={{0,4},{4,8},{8,12},{12,16},{16,20},{20,24},{24,28},{1,5},{5,9},{9,... | collective-permute-start | bytes 1572872 | tf_op jit(solution)/shard_map/ppermute | solution.py:16
  67.3 1.2 copy-start.2
  68.5 1.2 copy-start.3
  69.7 203.8 %copy-start = (s32[12288]{0:T(1024)S(1)}, s32[12288]{0:T(1024)}, u32[]{:S(2)}) copy-start(s32[12288]{0:T(1024)} %send_ref.1) | copy-start | bytes 147460
  69.7 203.8 %copy-start.1 = (s32[8192]{0:T(1024)S(1)}, s32[8192]{0:T(1024)}, u32[]{:S(2)}) copy-start(s32[8192]{0:T(1024)} %recv_ref.1) | copy-start | bytes 98308

commit v4 on v3

--- a/solution.py
+++ b/solution.py
@@ -16,28 +16,32 @@
     return lax.ppermute(block, axis, route)
 
 
-def compact_kernel(nb_ref, list_ref, pos_ref, *, absent):
-    offsets, block = nb_ref.shape
+def compact_kernel(nb_ref, list_ref, pos_ref, *, absent, block):
+    offsets, width = nb_ref.shape
     value = nb_ref[...]
     present = value != absent
-    lane = lax.broadcasted_iota(jnp.int32, (offsets, block), 1)
+    lane = lax.broadcasted_iota(jnp.int32, (offsets, width), 1) & (block - 1)
     before = lax.broadcasted_iota(jnp.int32, (block, block), 0)
     after = lax.broadcasted_iota(jnp.int32, (block, block), 1)
     triangle = jnp.where(before <= after, 1.0, 0.0).astype(jnp.bfloat16)
     ones = jnp.where(present, 1.0, 0.0).astype(jnp.bfloat16)
-    counted = jnp.dot(ones, triangle, preferred_element_type=jnp.float32).astype(jnp.int32)
-    pos = counted - 1
+    counted = [
+        jnp.dot(ones[:, at : at + block], triangle, preferred_element_type=jnp.float32)
+        for at in range(0, width, block)
+    ]
+    pos = jnp.concatenate(counted, axis=1).astype(jnp.int32) - 1
     pos_ref[...] = jnp.where(present, pos, -1)
     word = jnp.where(present, value + (lane - pos) * 16384 + (1 << 23), 0)
     for bit in range(block.bit_length() - 1):
         moves = (word & (16384 << bit)) != 0
-        moved = pltpu.roll(jnp.where(moves, word, 0), block - (1 << bit), 1)
+        moved = pltpu.roll(jnp.where(moves, word, 0), width - (1 << bit), 1)
         word = jnp.where(moves, 0, word) + moved
     list_ref[...] = jnp.where(word != 0, word & 16383, absent)
 
 
 def conv_kernel(
     list_ref,
+    next_ref,
     pos_ref,
     feat_ref,
     low_ref,
@@ -77,49 +81,61 @@
         at = 2 * pair + j
         return at + jnp.where(at >= middle, 1, 0)
 
-    def gather(pair, buf, base=0):
-        for j in range(2):
+    def gather(pair, buf, base=0, count=2, lists=list_ref):
+        for j in range(2 * count):
             k = offset_of(pair, j)
             for c in range(half):
-                buf[pl.ds(j * half + c, 1), :] = table[list_ref[k, base + c]]
-
-    def multiply(pair, buf, base=0):
-        products, spreads = [], []
-        for j in range(2):
-            k = offset_of(pair, j)
-            rows_in = buf[j * half : (j + 1) * half, :].astype(jnp.bfloat16)
-            products.append(
-                lax.dot_general(
-                    w_ref[k], rows_in, (((1,), (1,)), ((), ())), preferred_element_type=jnp.float32
+                buf[pl.ds(j * half + c, 1), :] = table[lists[k, base + c]]
+
+    def multiply(pair, buf, base=0, count=2):
+        total = jnp.zeros_like(acc_ref)
+        for i in range(count):
+            products, spreads = [], []
+            for j in range(2 * i, 2 * i + 2):
+                k = offset_of(pair, j)
+                rows_in = buf[j * half : (j + 1) * half, :].astype(jnp.bfloat16)
+                products.append(
+                    lax.dot_general(
+                        w_ref[k],
+                        rows_in,
+                        (((1,), (1,)), ((), ())),
+                        preferred_element_type=jnp.float32,
+                    )
                 )
-            )
-            wanted = pos_ref[pl.ds(k, 1), :] - base
-            spreads.append(jnp.where(slots == wanted, 1.0, 0.0).astype(jnp.bfloat16))
-        product = jnp.concatenate(products, axis=1)
-        high = product.astype(jnp.bfloat16)
-        low = (product - high.astype(jnp.float32)).astype(jnp.bfloat16)
-        both = jnp.concatenate([high, low], axis=0)
-        spread = jnp.concatenate(spreads, axis=0)
-        result = jnp.dot(both, spread, preferred_element_type=jnp.float32)
-        acc_ref[...] += result[:channels] + result[channels:]
+                wanted = pos_ref[pl.ds(k, 1), :] - base
+                spreads.append(jnp.where(slots == wanted, 1.0, 0.0).astype(jnp.bfloat16))
+            product = jnp.concatenate(products, axis=1)
+            high = product.astype(jnp.bfloat16)
+            low = (product - high.astype(jnp.float32)).astype(jnp.bfloat16)
+            both = jnp.concatenate([high, low], axis=0)
+            spread = jnp.concatenate(spreads, axis=0)
+            result = jnp.dot(both, spread, preferred_element_type=jnp.float32)
+            total += result[:channels] + result[channels:]
+        acc_ref[...] += total
 
     own = feat_ref[pl.ds(pl.multiple_of(step * block, block), block), :]
-    gather(0, buf_a)
+    pairs = middle
+
+    @pl.when(step == 0)
+    def _():
+        gather(0, buf_a, count=1)
+
     acc_ref[...] = lax.dot_general(
         w_ref[middle], own, (((1,), (1,)), ((), ())), preferred_element_type=jnp.float32
     )
-
-    pairs = middle
-
-    @pl.loop(0, pairs // 2)
+    gather(1, buf_b)
+    multiply(0, buf_a, count=1)
+
+    @pl.loop(0, (pairs - 3) // 4)
     def _(p):
-        first = 2 * p
-        gather(first + 1, buf_b)
-        multiply(first, buf_a)
+        first = 1 + 4 * p
         gather(first + 2, buf_a)
-        multiply(first + 1, buf_b)
-
-    multiply(pairs - 1, buf_a)
+        multiply(first, buf_b)
+        gather(first + 4, buf_b)
+        multiply(first + 2, buf_a)
+
+    gather(pairs - 2, buf_a)
+    multiply(pairs - 4, buf_b)
 
     crowded = jnp.int32(0)
     for k in range(offsets):
@@ -137,9 +153,11 @@
 
             @pl.when(more)
             def _():
-                gather(p, buf_a, half)
-                multiply(p, buf_a, half)
-
+                gather(p, buf_b, half, 1)
+                multiply(p, buf_b, half, 1)
+
+    multiply(pairs - 2, buf_a)
+    gather(0, buf_a, count=1, lists=next_ref)
     summed = acc_ref[...].T
     centered = summed - jnp.mean(summed, axis=-1, keepdims=True)
     spread_sq = jnp.mean(centered * centered, axis=-1, keepdims=True)
@@ -150,16 +168,17 @@
 
 def compact(columns, absent):
     offsets, rows = columns.shape
-    spec = pl.BlockSpec((offsets, BLOCK), lambda i: (0, i))
+    width = 8 * BLOCK
+    spec = pl.BlockSpec((offsets, width), lambda i: (0, i))
     shape = jax.ShapeDtypeStruct((offsets, rows), jnp.int32)
     return pl.pallas_call(
-        functools.partial(compact_kernel, absent=absent),
-        grid=(rows // BLOCK,),
+        functools.partial(compact_kernel, absent=absent, block=BLOCK),
+        grid=(rows // width,),
         out_shape=(shape, shape),
         in_specs=[spec],
         out_specs=(spec, spec),
         cost_estimate=pl.CostEstimate(
-            flops=100 * rows * offsets, bytes_accessed=12 * rows * offsets, transcendentals=0
+            flops=0, bytes_accessed=200 * rows * offsets, transcendentals=0
         ),
     )(columns)
 
@@ -170,12 +189,16 @@
     offsets = lists.shape[0]
     block = BLOCK
     whole = pl.BlockSpec(memory_space=pltpu.VMEM)
+    last = rows // block - 1
     return pl.pallas_call(
         conv_kernel,
         grid=(rows // block,),
         out_shape=jax.ShapeDtypeStruct((rows, channels), jnp.bfloat16),
         in_specs=[
             pl.BlockSpec((offsets, block), lambda i: (0, i), memory_space=pltpu.SMEM),
+            pl.BlockSpec(
+                (offsets, block), lambda i: (0, jnp.minimum(i + 1, last)), memory_space=pltpu.SMEM
+            ),
             pl.BlockSpec((offsets, block), lambda i: (0, i)),
             whole,
             whole,
@@ -187,8 +210,8 @@
         out_specs=pl.BlockSpec((block, channels), lambda i: (i, 0)),
         scratch_shapes=[
             pltpu.VMEM((rows + 2 * halo + 8, channels), jnp.float32),
-            pltpu.VMEM((block, channels), jnp.float32),
-            pltpu.VMEM((block, channels), jnp.float32),
+            pltpu.VMEM((2 * block, channels), jnp.float32),
+            pltpu.VMEM((2 * block, channels), jnp.float32),
             pltpu.VMEM((channels, block), jnp.float32),
         ],
         compiler_params=pltpu.CompilerParams(vmem_limit_bytes=48 * 1024 * 1024),
@@ -197,7 +220,7 @@
             bytes_accessed=8 * rows * channels,
             transcendentals=rows * channels,
         ),
-    )(lists, places, features, from_lower, from_upper, weights, gain, shift)
+    )(lists, lists, places, features, from_lower, from_upper, weights, gain, shift)
 
 
 def relay_kernel(

time: 332 us -> 258 us (0.78)
  Pallas kernels: 283 us -> 211 us
    pallas_call x1, Pallas kernels: 204 us -> 153 us  [conv_block(): pl.pallas_call(conv_kernel, grid=(rows // block,), out_shape=jax.ShapeDty...]
    pallas_call x1, Pallas kernels: 25 us -> 5.49 us  [compact(): pl.pallas_call(functools.partial(compact_kernel, absent=absent, block=BLO...]
  transfers between devices with their start and end apart: 2 -> 2, of which waited for: 0 -> 0; matrix products, arithmetic and copies ran while one was open for 2% -> 3% of each run, Pallas kernels for 8% -> 2%
where the time goes in v4:
time: 258 us; the launch traced here: 257 us
  Pallas kernels  211 us (82%)
  blocking collectives  19 us (7%)
  local copies, waits for them, and re-layouts  17.6 us (7%)
  starting transfers between devices  6.42 us (2%)
  other arithmetic  2.92 us (1%)
    pallas_call x1, Pallas kernels, conv_block(): pl.pallas_call(conv_kernel, grid=(rows // block,), out_shape=jax.ShapeDty...  153 us
    pallas_call x1, Pallas kernels, relay(): pl.pallas_call(functools.partial(relay_kernel, axis=axis, count=count), o...  52 us
    all_gather x1, blocking collectives, body(): lax.all_gather(kernel.transpose(0, 2, 1), 'grp', axis=1, tiled=True)  19 us
    gather x1, local copies, waits for them, and re-layouts, body(): downward = jnp.take(features, send_low, axis=0)  7.6 us
    ppermute x2, starting transfers between devices, shifted(): return lax.ppermute(block, axis, route)  6.42 us
    gather x1, local copies, waits for them, and re-layouts, body(): upward = jnp.take(features, send_high, axis=0)  6.18 us
    pallas_call x1, Pallas kernels, compact(): pl.pallas_call(functools.partial(compact_kernel, absent=absent, block=BLO...  5.49 us
  transfers between devices with their start and end apart: 2, of which 0 were waited for; matrix products, arithmetic and copies ran while one was open for 3% of the time, Pallas kernels for 2%

profile of v4, /device:TPU:1, one launch (start us, length us, event | category | flops | bytes accessed | tf_op | source)
XLA Modules:
  0.0 257.0 jit_solution(18036370951593738698)
XLA Ops:
  0.0 0.7 compare_and_fusion
  0.7 0.7 fusion.1
  1.4 0.0 copy-start.8
  1.4 0.0 copy-start.6
  1.4 7.6 %gather_fusion.1 = bf16[2048,128]{1,0:T(8,128)(2,1)S(1)} fusion(bf16[8192,128]{1,0:T(8,128)(2,1)} %feat_ref.1, s32[2048]{0:T(1024)S(1)} %fusion.1), kind=kCustom, calls=%fused_computation.1.clone | custom fusion | bytes 1056768 | tf_op jit(solution)/shard_map/jit(_take)/gather | solution.py:366
  9.0 1.2 broadcast_select_fusion
  10.2 2.0 collective-permute-start.1
  12.1 0.0 copy-done.8
  12.2 0.0 copy-done.6
  12.2 6.2 %gather_fusion = bf16[2048,128]{1,0:T(8,128)(2,1)S(1)} fusion(bf16[8192,128]{1,0:T(8,128)(2,1)S(1)} %copy-done.6, s32[2048]{0:T(1024)S(1)} %fusion), kind=kCustom, calls=%fused_computation.clone | custom fusion | bytes 1056768 | tf_op jit(solution)/shard_map/jit(_take)/gather | solution.py:365
  18.4 0.0 copy-start.7
  18.4 0.0 copy-start.4
  18.4 0.0 copy-start.5
  18.4 0.3 broadcast_select_fusion.1
  18.8 4.5 %collective-permute-start = (bf16[2048,128]{1,0:T(8,128)(2,1)S(1)}, bf16[2048,128]{1,0:T(8,128)(2,1)S(1)}, u32[]{:S(2)}, u32[]{:S(2)}) collective-permute-start(bf16[2048,128]{1,0:T(8,128)(2,1)S(1)} %broadcast_select_fusion.1), channel_id=1, source_target_pairs={{0,4},{4,8},{8,12},{12,16},{16,20},{20,24},{24,28},{1,5},{5,9},{9,... | collective-permute-start | bytes 1572872 | tf_op jit(solution)/shard_map/ppermute | solution.py:16
  23.2 5.5 %shard_map.91 = (s32[27,8192]{1,0:T(8,128)}, s32[27,8192]{1,0:T(8,128)}) custom-call(s32[27,8192]{1,0:T(8,128)} %bitcast.6), custom_call_target="tpu_custom_call" | custom-call | bytes 44236800 | tf_op jit(solution)/shard_map/pallas_call | solution.py:174
  28.7 0.0 copy-done.7
  28.7 19.0 %all_gather.3.w_ref = bf16[27,128,128]{2,1,0:T(8,128)(2,1)S(1)} all-gather(bf16[27,32,128]{2,1,0:T(8,128)(2,1)S(1)} %bitcast.7), channel_id=1, replica_groups=mesh['brick'=8,'grp'=4] {'grp'}, dimensions={1}, use_global_device_ids=true | all-gather | bytes 1105920 | tf_op jit(solution)/shard_map/all_gather | solution.py:364
  47.7 0.0 collective-permute-done.1.up_ref
  47.7 0.0 collective-permute-done.low_ref
  47.7 0.0 copy-done.4
  47.7 0.0 copy-done.5
  47.7 0.0 copy-start.2
  47.8 1.2 copy-done.2
  49.0 0.0 copy-start.3
  49.0 1.2 copy-done.3
  50.2 0.0 copy-start
  50.2 0.0 copy-start.1
  50.2 153.4 %shard_map.92.rows_ref = bf16[8192,128]{1,0:T(8,128)(2,1)S(1)} custom-call(s32[27,8192]{1,0:T(8,128)S(1)} %copy-done.2, s32[27,8192]{1,0:T(8,128)S(1)} %copy-done.2, s32[27,8192]{1,0:T(8,128)S(1)} %copy-done.3, bf16[8192,128]{1,0:T(8,128)(2,1)} %feat_ref.1, bf16[2048,128]{1,0:T(8,128)(2,1)S(1)} %collective-permute-done.low_ref, ...), custom_call_target="tpu_custom_call" | custom-call | flops 7247757312 | bytes 8388608 | tf_op jit(solution)/shard_map/pallas_call | solution.py:193
  203.7 0.0 copy-done
  203.7 0.0 copy-done.1
  203.7 52.0 %shard_map.93 = bf16[8192,128]{1,0:T(8,128)(2,1)S(1)} custom-call(s32[12288]{0:T(1024)S(1)} %copy-done, s32[8192]{0:T(1024)S(1)} %copy-done.1, bf16[8192,128]{1,0:T(8,128)(2,1)S(1)} %shard_map.92.rows_ref), custom_call_target="tpu_custom_call" | custom-call | tf_op jit(solution)/shard_map/pallas_call | solution.py:340
  255.7 1.3 copy.11
  (2 shorter events, 0.0 us)
Async XLA Ops:
  1.4 10.7 %copy-start.8 = (s32[2048]{0:T(1024)S(1)}, s32[2048]{0:T(1024)}, u32[]{:S(2)}) copy-start(s32[2048]{0:T(1024)} %param.14) | copy-start | bytes 24580
  1.4 10.8 %copy-start.6 = (bf16[8192,128]{1,0:T(8,128)(2,1)S(1)}, bf16[8192,128]{1,0:T(8,128)(2,1)}, u32[]{:S(2)}) copy-start(bf16[8192,128]{1,0:T(8,128)(2,1)} %feat_ref.1) | copy-start | bytes 6291460
  10.2 37.5 %collective-permute-start.1 = (bf16[2048,128]{1,0:T(8,128)(2,1)}, bf16[2048,128]{1,0:T(8,128)(2,1)S(1)}, u32[]{:S(2)}, u32[]{:S(2)}) collective-permute-start(bf16[2048,128]{1,0:T(8,128)(2,1)} %broadcast_select_fusion), channel_id=1, source_target_pairs={{4,0},{8,4},{12,8},{16,12},{20,16},{24,20},{28,24},{5,1},{9,5},{13... | collective-permute-start | bytes 1572872 | tf_op jit(solution)/shard_map/ppermute | solution.py:16
  18.4 10.4 %copy-start.7 = (bf16[27,128,32]{1,2,0:T(8,128)(2,1)S(1)}, bf16[27,128,32]{1,2,0:T(8,128)(2,1)}, u32[]{:S(2)}) copy-start(bf16[27,128,32]{1,2,0:T(8,128)(2,1)} %param.17) | copy-start | bytes 663556
  18.4 29.3 %copy-start.4 = (f32[128]{0:T(128)S(1)}, f32[128]{0:T(128)}, u32[]{:S(2)}) copy-start(f32[128]{0:T(128)} %param.18) | copy-start | bytes 1540
  18.4 29.3 %copy-start.5 = (f32[128]{0:T(128)S(1)}, f32[128]{0:T(128)}, u32[]{:S(2)}) copy-start(f32[128]{0:T(128)} %param.19) | copy-start | bytes 1540
  18.8 29.0 %collective-permute-start = (bf16[2048,128]{1,0:T(8,128)(2,1)S(1)}, bf16[2048,128]{1,0:T(8,128)(2,1)S(1)}, u32[]{:S(2)}, u32[]{:S(2)}) collective-permute-start(bf16[2048,128]{1,0:T(8,128)(2,1)S(1)} %broadcast_select_fusion.1), channel_id=1, source_target_pairs={{0,4},{4,8},{8,12},{12,16},{16,20},{20,24},{24,28},{1,5},{5,9},{9,... | collective-permute-start | bytes 1572872 | tf_op jit(solution)/shard_map/ppermute | solution.py:16
  47.7 1.2 copy-start.2
  49.0 1.2 copy-start.3
  50.2 153.5 %copy-start = (s32[12288]{0:T(1024)S(1)}, s32[12288]{0:T(1024)}, u32[]{:S(2)}) copy-start(s32[12288]{0:T(1024)} %send_ref.1) | copy-start | bytes 147460
  50.2 153.5 %copy-start.1 = (s32[8192]{0:T(1024)S(1)}, s32[8192]{0:T(1024)}, u32[]{:S(2)}) copy-start(s32[8192]{0:T(1024)} %recv_ref.1) | copy-start | bytes 98308

commit v5 on v4

--- a/solution.py
+++ b/solution.py
@@ -14,6 +14,46 @@
     devices = range(lax.axis_size(axis))
     route = [(i - distance, i) for i in devices if i - distance in devices]
     return lax.ppermute(block, axis, route)
+
+
+def pick_kernel(high_ref, low_ref, feat_ref, upward_ref, downward_ref, table_ref, stage_ref):
+    rows, channels = feat_ref.shape
+    chunk = stage_ref.shape[0]
+    table = table_ref.reshape(rows, 1, channels)
+
+    @pl.loop(0, rows // chunk)
+    def _(i):
+        at = pl.ds(pl.multiple_of(i * chunk, chunk), chunk)
+        table_ref[at, :] = feat_ref[at, :].astype(jnp.float32)
+
+    for index_ref, into_ref in ((high_ref, upward_ref), (low_ref, downward_ref)):
+
+        @pl.loop(0, into_ref.shape[0] // chunk)
+        def _(i, index_ref=index_ref, into_ref=into_ref):
+            first = pl.multiple_of(i * chunk, chunk)
+            for c in range(chunk):
+                stage_ref[pl.ds(c, 1), :] = table[index_ref[first + c]]
+            into_ref[pl.ds(first, chunk), :] = stage_ref[...].astype(jnp.bfloat16)
+
+
+def pick_halo(features, send_high, send_low):
+    rows, channels = features.shape
+    halo = send_high.shape[0]
+    chunk = 256
+    whole = pl.BlockSpec(memory_space=pltpu.VMEM)
+    scalars = pl.BlockSpec(memory_space=pltpu.SMEM)
+    shape = jax.ShapeDtypeStruct((halo, channels), jnp.bfloat16)
+    return pl.pallas_call(
+        pick_kernel,
+        out_shape=(shape, shape),
+        in_specs=[scalars, scalars, whole],
+        out_specs=(whole, whole),
+        scratch_shapes=[
+            pltpu.VMEM((rows, channels), jnp.float32),
+            pltpu.VMEM((chunk, channels), jnp.float32),
+        ],
+        compiler_params=pltpu.CompilerParams(vmem_limit_bytes=16 * 1024 * 1024),
+    )(send_high, send_low, features)
 
 
 def compact_kernel(nb_ref, list_ref, pos_ref, *, absent, block):
@@ -362,8 +402,7 @@
 ):
     row_count, channels = features.shape
     weights = lax.all_gather(kernel.transpose(0, 2, 1), "grp", axis=1, tiled=True)
-    upward = jnp.take(features, send_high, axis=0)
-    downward = jnp.take(features, send_low, axis=0)
+    upward, downward = pick_halo(features, send_high, send_low)
     from_lower = shifted(upward, "brick", 1)
     from_upper = shifted(downward, "brick", -1)
     lists, places = compact(neighbors.T, row_count + 2 * send_low.shape[0])

time: 258 us -> 251 us (0.973)
  local copies, waits for them, and re-layouts: 17.6 us -> 6.77 us
  Pallas kernels: 211 us -> 219 us
  other arithmetic: 2.92 us -> 0 us
    gather x2 -> x0, local copies, waits for them, and re-layouts: 13.8 us -> none  [the longest x1 7.6 us: body(): downward = jnp.take(features, send_low, axis=0)]
    pallas_call x0 -> x1, Pallas kernels: none -> 4.72 us  [pick_halo(): pl.pallas_call(pick_kernel, out_shape=(shape, shape), in_specs=[scalars,...]
    pallas_call x1, Pallas kernels: 52 us -> 55.8 us  [relay(): pl.pallas_call(functools.partial(relay_kernel, axis=axis, count=count), o...]
    unnamed x19 -> x21, local copies, waits for them, and re-layouts: 3.8 us -> 6.77 us
  transfers between devices with their start and end apart: 2 -> 2, of which waited for: 0 -> 0; matrix products, arithmetic and copies ran while one was open for 3% -> 0% of each run, Pallas kernels for 2% -> 2%
where the time goes in v5:
time: 251 us
  Pallas kernels  219 us (87%)
  blocking collectives  18.8 us (7%)
  local copies, waits for them, and re-layouts  6.77 us (3%)
  starting transfers between devices  6.43 us (3%)
    pallas_call x1, Pallas kernels, conv_block(): pl.pallas_call(conv_kernel, grid=(rows // block,), out_shape=jax.ShapeDty...  153 us
    pallas_call x1, Pallas kernels, relay(): pl.pallas_call(functools.partial(relay_kernel, axis=axis, count=count), o...  55.8 us
    all_gather x1, blocking collectives, body(): lax.all_gather(kernel.transpose(0, 2, 1), 'grp', axis=1, tiled=True)  18.8 us
    unnamed x21, local copies, waits for them, and re-layouts  6.77 us
    ppermute x2, starting transfers between devices, shifted(): return lax.ppermute(block, axis, route)  6.43 us
    pallas_call x1, Pallas kernels, compact(): pl.pallas_call(functools.partial(compact_kernel, absent=absent, block=BLO...  5.49 us
  transfers between devices with their start and end apart: 2, of which 0 were waited for; matrix products, arithmetic and copies ran while one was open for 0% of the time, Pallas kernels for 2%

profile of v5, /device:TPU:1, one launch (start us, length us, event | category | flops | bytes accessed | tf_op | source)
XLA Modules:
  0.0 250.7 jit_solution(15977241790202542953)
XLA Ops:
  0.0 0.0 copy-start
  0.0 1.6 copy-done
  1.6 0.0 copy-start.3
  1.6 0.7 copy-done.3
  2.3 0.0 copy-start.4
  2.3 0.7 copy-done.4
  3.0 0.0 copy-start.9
  3.0 0.0 copy-start.7
  3.0 0.0 copy-start.8
  3.0 4.7 %shard_map.92 = (bf16[2048,128]{1,0:T(8,128)(2,1)S(1)}, bf16[2048,128]{1,0:T(8,128)(2,1)S(1)}) custom-call(s32[2048]{0:T(1024)S(1)} %copy-done.3, s32[2048]{0:T(1024)S(1)} %copy-done.4, bf16[8192,128]{1,0:T(8,128)(2,1)S(1)} %copy-done), custom_call_target="tpu_custom_call" | custom-call | tf_op jit(solution)/shard_map/pallas_call | solution.py:46
  7.7 4.5 %collective-permute-start = (bf16[2048,128]{1,0:T(8,128)(2,1)S(1)}, bf16[2048,128]{1,0:T(8,128)(2,1)S(1)}, u32[]{:S(2)}, u32[]{:S(2)}) collective-permute-start(bf16[2048,128]{1,0:T(8,128)(2,1)S(1)} %get-tuple-element.11), channel_id=1, source_target_pairs={{0,4},{4,8},{8,12},{12,16},{16,20},{20,24},{24,28},{1,5},{5,9},{9,... | collective-permute-start | bytes 1572872 | tf_op jit(solution)/shard_map/ppermute | solution.py:16
  12.2 1.9 collective-permute-start.1
  14.2 5.5 %shard_map.91 = (s32[27,8192]{1,0:T(8,128)}, s32[27,8192]{1,0:T(8,128)}) custom-call(s32[27,8192]{1,0:T(8,128)} %bitcast.6), custom_call_target="tpu_custom_call" | custom-call | bytes 44236800 | tf_op jit(solution)/shard_map/pallas_call | solution.py:214
  19.7 0.0 copy-done.9
  19.7 18.8 %all_gather.3.w_ref = bf16[27,128,128]{2,1,0:T(8,128)(2,1)S(1)} all-gather(bf16[27,32,128]{2,1,0:T(8,128)(2,1)S(1)} %bitcast.7), channel_id=1, replica_groups=mesh['brick'=8,'grp'=4] {'grp'}, dimensions={1}, use_global_device_ids=true | all-gather | bytes 1105920 | tf_op jit(solution)/shard_map/all_gather | solution.py:404
  38.5 0.0 collective-permute-done.low_ref
  38.5 0.0 collective-permute-done.1.up_ref
  38.5 0.0 copy-done.7
  38.5 0.0 copy-done.8
  38.5 0.0 copy-start.5
  38.5 1.2 copy-done.5
  39.8 0.0 copy-start.6
  39.8 1.2 copy-done.6
  41.0 0.0 copy-start.1
  41.0 0.0 copy-start.2
  41.0 152.6 %shard_map.93.rows_ref = bf16[8192,128]{1,0:T(8,128)(2,1)S(1)} custom-call(s32[27,8192]{1,0:T(8,128)S(1)} %copy-done.5, s32[27,8192]{1,0:T(8,128)S(1)} %copy-done.5, s32[27,8192]{1,0:T(8,128)S(1)} %copy-done.6, bf16[8192,128]{1,0:T(8,128)(2,1)} %feat_ref.3, bf16[2048,128]{1,0:T(8,128)(2,1)S(1)} %collective-permute-done.low_ref, ...), custom_call_target="tpu_custom_call" | custom-call | flops 7247757312 | bytes 8388608 | tf_op jit(solution)/shard_map/pallas_call | solution.py:233
  193.5 0.0 copy-done.1
  193.6 0.0 copy-done.2
  193.6 55.8 %shard_map.94 = bf16[8192,128]{1,0:T(8,128)(2,1)S(1)} custom-call(s32[12288]{0:T(1024)S(1)} %copy-done.1, s32[8192]{0:T(1024)S(1)} %copy-done.2, bf16[8192,128]{1,0:T(8,128)(2,1)S(1)} %shard_map.93.rows_ref), custom_call_target="tpu_custom_call" | custom-call | tf_op jit(solution)/shard_map/pallas_call | solution.py:380
  249.4 1.3 copy.11
Async XLA Ops:
  0.0 1.6 copy-start
  1.6 0.7 copy-start.3
  2.3 0.7 copy-start.4
  3.0 16.7 %copy-start.9 = (bf16[27,128,32]{1,2,0:T(8,128)(2,1)S(1)}, bf16[27,128,32]{1,2,0:T(8,128)(2,1)}, u32[]{:S(2)}) copy-start(bf16[27,128,32]{1,2,0:T(8,128)(2,1)} %param.15) | copy-start | bytes 663556
  3.0 35.5 %copy-start.7 = (f32[128]{0:T(128)S(1)}, f32[128]{0:T(128)}, u32[]{:S(2)}) copy-start(f32[128]{0:T(128)} %param.16) | copy-start | bytes 1540
  3.0 35.5 %copy-start.8 = (f32[128]{0:T(128)S(1)}, f32[128]{0:T(128)}, u32[]{:S(2)}) copy-start(f32[128]{0:T(128)} %param.17) | copy-start | bytes 1540
  7.7 30.8 %collective-permute-start = (bf16[2048,128]{1,0:T(8,128)(2,1)S(1)}, bf16[2048,128]{1,0:T(8,128)(2,1)S(1)}, u32[]{:S(2)}, u32[]{:S(2)}) collective-permute-start(bf16[2048,128]{1,0:T(8,128)(2,1)S(1)} %get-tuple-element.11), channel_id=1, source_target_pairs={{0,4},{4,8},{8,12},{12,16},{16,20},{20,24},{24,28},{1,5},{5,9},{9,... | collective-permute-start | bytes 1572872 | tf_op jit(solution)/shard_map/ppermute | solution.py:16
  12.2 26.3 %collective-permute-start.1 = (bf16[2048,128]{1,0:T(8,128)(2,1)S(1)}, bf16[2048,128]{1,0:T(8,128)(2,1)S(1)}, u32[]{:S(2)}, u32[]{:S(2)}) collective-permute-start(bf16[2048,128]{1,0:T(8,128)(2,1)S(1)} %get-tuple-element.12), channel_id=1, source_target_pairs={{4,0},{8,4},{12,8},{16,12},{20,16},{24,20},{28,24},{5,1},{9,5},{13... | collective-permute-start | bytes 1572872 | tf_op jit(solution)/shard_map/ppermute | solution.py:16
  38.5 1.2 copy-start.5
  39.8 1.2 copy-start.6
  41.0 152.6 %copy-start.1 = (s32[12288]{0:T(1024)S(1)}, s32[12288]{0:T(1024)}, u32[]{:S(2)}) copy-start(s32[12288]{0:T(1024)} %send_ref.1) | copy-start | bytes 147460
  41.0 152.6 %copy-start.2 = (s32[8192]{0:T(1024)S(1)}, s32[8192]{0:T(1024)}, u32[]{:S(2)}) copy-start(s32[8192]{0:T(1024)} %recv_ref.1) | copy-start | bytes 98308

commit v6 on v5

--- a/solution.py
+++ b/solution.py
@@ -86,10 +86,14 @@
     feat_ref,
     low_ref,
     up_ref,
-    w_ref,
+    place_ref,
+    mine_ref,
+    got_ref,
+    passed_ref,
     gain_ref,
     shift_ref,
     out_ref,
+    w_ref,
     tab_ref,
     buf_a,
     buf_b,
@@ -104,6 +108,8 @@
     absent = rows + 2 * halo
     table = tab_ref.reshape(tab_ref.shape[0], 1, channels)
     slots = lax.broadcasted_iota(jnp.int32, (half, block), 0)
+    slots = slots.astype(jnp.float32).astype(jnp.bfloat16)
+    one, zero = jnp.bfloat16(1), jnp.bfloat16(0)
 
     @pl.when(step == 0)
     def _():
@@ -116,6 +122,18 @@
                 tab_ref[pl.ds(start + at, chunk), :] = src[pl.ds(at, chunk), :].astype(jnp.float32)
 
         tab_ref[pl.ds(absent, 8), :] = jnp.zeros((8, channels), jnp.float32)
+
+        columns = mine_ref.shape[1]
+        part = columns // 2
+        groups = got_ref.shape[0] + 1
+        group, core = place_ref[0], place_ref[1]
+        at = pl.multiple_of(group * columns, columns)
+        w_ref[:, pl.ds(at, columns), :] = mine_ref[...]
+        for j in range(groups - 1):
+            source = lax.rem(group - j - 1 + groups, groups)
+            for ref, which in ((got_ref, core), (passed_ref, 1 - core)):
+                at = pl.multiple_of(source * columns + which * part, part)
+                w_ref[:, pl.ds(at, part), :] = ref[j]
 
     def offset_of(pair, j):
         at = 2 * pair + j
@@ -128,30 +146,24 @@
                 buf[pl.ds(j * half + c, 1), :] = table[lists[k, base + c]]
 
     def multiply(pair, buf, base=0, count=2):
-        total = jnp.zeros_like(acc_ref)
-        for i in range(count):
-            products, spreads = [], []
-            for j in range(2 * i, 2 * i + 2):
-                k = offset_of(pair, j)
-                rows_in = buf[j * half : (j + 1) * half, :].astype(jnp.bfloat16)
-                products.append(
-                    lax.dot_general(
-                        w_ref[k],
-                        rows_in,
-                        (((1,), (1,)), ((), ())),
-                        preferred_element_type=jnp.float32,
-                    )
+        products, spreads = [], []
+        for j in range(2 * count):
+            k = offset_of(pair, j)
+            rows_in = buf[j * half : (j + 1) * half, :].astype(jnp.bfloat16)
+            products.append(
+                lax.dot_general(
+                    w_ref[k], rows_in, (((1,), (1,)), ((), ())), preferred_element_type=jnp.float32
                 )
-                wanted = pos_ref[pl.ds(k, 1), :] - base
-                spreads.append(jnp.where(slots == wanted, 1.0, 0.0).astype(jnp.bfloat16))
-            product = jnp.concatenate(products, axis=1)
-            high = product.astype(jnp.bfloat16)
-            low = (product - high.astype(jnp.float32)).astype(jnp.bfloat16)
-            both = jnp.concatenate([high, low], axis=0)
-            spread = jnp.concatenate(spreads, axis=0)
-            result = jnp.dot(both, spread, preferred_element_type=jnp.float32)
-            total += result[:channels] + result[channels:]
-        acc_ref[...] += total
+            )
+            wanted = (pos_ref[pl.ds(k, 1), :] - base).astype(jnp.float32).astype(jnp.bfloat16)
+            spreads.append(jnp.where(slots == wanted, one, zero))
+        product = jnp.concatenate(products, axis=1)
+        high = product.astype(jnp.bfloat16)
+        low = (product - high.astype(jnp.float32)).astype(jnp.bfloat16)
+        both = jnp.concatenate([high, low], axis=0)
+        spread = jnp.concatenate(spreads, axis=0)
+        result = jnp.dot(both, spread, preferred_element_type=jnp.float32)
+        acc_ref[...] += result[:channels] + result[channels:]
 
     own = feat_ref[pl.ds(pl.multiple_of(step * block, block), block), :]
     pairs = middle
@@ -224,6 +236,7 @@
 
 
 def conv_block(features, from_lower, from_upper, lists, places, weights, gain, shift):
+    place, mine, got, passed = weights
     rows, channels = features.shape
     halo = from_lower.shape[0]
     offsets = lists.shape[0]
@@ -243,12 +256,16 @@
             whole,
             whole,
             whole,
+            pl.BlockSpec(memory_space=pltpu.SMEM),
+            whole,
+            whole,
             whole,
             whole,
             whole,
         ],
         out_specs=pl.BlockSpec((block, channels), lambda i: (i, 0)),
         scratch_shapes=[
+            pltpu.VMEM((offsets, channels, channels), jnp.bfloat16),
             pltpu.VMEM((rows + 2 * halo + 8, channels), jnp.float32),
             pltpu.VMEM((2 * block, channels), jnp.float32),
             pltpu.VMEM((2 * block, channels), jnp.float32),
@@ -260,7 +277,20 @@
             bytes_accessed=8 * rows * channels,
             transcendentals=rows * channels,
         ),
-    )(lists, lists, places, features, from_lower, from_upper, weights, gain, shift)
+    )(
+        lists,
+        lists,
+        places,
+        features,
+        from_lower,
+        from_upper,
+        place,
+        mine,
+        got,
+        passed,
+        gain,
+        shift,
+    )
 
 
 def relay_kernel(
@@ -397,11 +427,26 @@
     )(send_slot, recv_slot, blended)
 
 
+def spread_weights(mine):
+    slabs, groups = lax.axis_size("brick"), lax.axis_size("grp")
+    core = lax.rem(lax.axis_index("brick"), 2)
+    part = mine.shape[1] // 2
+    half = lax.dynamic_slice_in_dim(mine, core * part, part, axis=1)
+    got = [
+        lax.ppermute(half, "grp", [(i, (i + j) % groups) for i in range(groups)])
+        for j in range(1, groups)
+    ]
+    got = jnp.stack(got)
+    passed = lax.ppermute(got, "brick", [(i, i ^ 1) for i in range(slabs)])
+    place = jnp.stack([lax.axis_index("grp"), core]).astype(jnp.int32)
+    return place, mine, got, passed
+
+
 def body(
     features, neighbors, send_low, send_high, send_slot, recv_slot, kernel, norm_gain, norm_shift
 ):
     row_count, channels = features.shape
-    weights = lax.all_gather(kernel.transpose(0, 2, 1), "grp", axis=1, tiled=True)
+    weights = spread_weights(kernel.transpose(0, 2, 1))
     upward, downward = pick_halo(features, send_high, send_low)
     from_lower = shifted(upward, "brick", 1)
     from_upper = shifted(downward, "brick", -1)

time: 251 us -> 241 us (0.960)
  blocking collectives: 18.8 us -> 0 us
  waiting for transfers between devices: 0.01 us -> 5.72 us
  starting transfers between devices: 6.43 us -> 11.1 us
  Pallas kernels: 219 us -> 215 us
    all_gather x1 -> x0, blocking collectives: 18.8 us -> none  [body(): lax.all_gather(kernel.transpose(0, 2, 1), 'grp', axis=1, tiled=True)]
    ppermute x2, waiting for transfers between devices: 0.01 us -> 5.71 us  [shifted(): return lax.ppermute(block, axis, route)]
    pallas_call x1, Pallas kernels: 55.8 us -> 50.6 us  [relay(): pl.pallas_call(functools.partial(relay_kernel, axis=axis, count=count), o...]
    ppermute x0 -> x4, starting transfers between devices: none -> 4.68 us  [the longest x3 4.6 us: spread_weights(): lax.ppermute(half, 'grp', [(i, (i + j) % groups) for i in range(groups)])]
  transfers between devices with their start and end apart: 2 -> 6, of which waited for: 0 -> 1; matrix products, arithmetic and copies ran while one was open for 0% -> 0% of each run, Pallas kernels for 2% -> 4%
where the time goes in v6:
time: 241 us; the launch traced here: 240 us
  Pallas kernels  215 us (89%)
  starting transfers between devices  11.1 us (5%)
  local copies, waits for them, and re-layouts  7.73 us (3%)
  waiting for transfers between devices  5.72 us (2%)
    pallas_call x1, Pallas kernels, conv_block(): pl.pallas_call(conv_kernel, grid=(rows // block,), out_shape=jax.ShapeDty...  154 us
    pallas_call x1, Pallas kernels, relay(): pl.pallas_call(functools.partial(relay_kernel, axis=axis, count=count), o...  50.6 us
    unnamed x21, local copies, waits for them, and re-layouts  6.77 us
    ppermute x2, starting transfers between devices, shifted(): return lax.ppermute(block, axis, route)  6.44 us
    ppermute x2, waiting for transfers between devices, shifted(): return lax.ppermute(block, axis, route)  5.71 us
    pallas_call x1, Pallas kernels, compact(): pl.pallas_call(functools.partial(compact_kernel, absent=absent, block=BLO...  5.49 us
  transfers between devices with their start and end apart: 6, of which 1 were waited for; matrix products, arithmetic and copies ran while one was open for 0% of the time, Pallas kernels for 4%

profile of v6, /device:TPU:1, one launch (start us, length us, event | category | flops | bytes accessed | tf_op | source)
XLA Modules:
  0.0 239.5 jit_solution(17514568727449607484)
XLA Ops:
  0.0 0.0 copy-start.1
  0.0 0.0 copy-start.9
  0.0 0.0 copy-start.8
  0.0 1.0 dynamic-slice_bitcast_fusion
  1.0 4.2 %collective-permute-start.4 = (bf16[27,16,128]{2,1,0:T(8,128)(2,1)S(1)}, bf16[27,16,128]{2,1,0:T(8,128)(2,1)S(1)}, u32[]{:S(2)}, u32[]{:S(2)}) collective-permute-start(bf16[27,16,128]{2,1,0:T(8,128)(2,1)S(1)} %dynamic-slice_bitcast_fusion), channel_id=1, source_target_pairs={{0,3},{1,0},{2,1},{3,2},{4,7},{5,4},{6,5},{7,6},{8,11},{9,8},{10,9... | collective-permute-start | bytes 331784 | tf_op jit(solution)/shard_map/ppermute | solution.py:436
  5.1 0.0 collective-permute-start.3
  5.1 0.5 collective-permute-start.2
  5.6 0.0 copy-start
  5.6 1.6 copy-done
  7.2 0.0 copy-start.4
  7.2 0.7 copy-done.4
  7.9 0.0 copy-start.5
  7.9 0.7 copy-done.5
  8.6 4.7 %shard_map.92 = (bf16[2048,128]{1,0:T(8,128)(2,1)S(1)}, bf16[2048,128]{1,0:T(8,128)(2,1)S(1)}) custom-call(s32[2048]{0:T(1024)S(1)} %copy-done.4, s32[2048]{0:T(1024)S(1)} %copy-done.5, bf16[8192,128]{1,0:T(8,128)(2,1)S(1)} %copy-done), custom_call_target="tpu_custom_call" | custom-call | tf_op jit(solution)/shard_map/pallas_call | solution.py:46
  13.3 4.5 %collective-permute-start = (bf16[2048,128]{1,0:T(8,128)(2,1)S(1)}, bf16[2048,128]{1,0:T(8,128)(2,1)S(1)}, u32[]{:S(2)}, u32[]{:S(2)}) collective-permute-start(bf16[2048,128]{1,0:T(8,128)(2,1)S(1)} %get-tuple-element.11), channel_id=1, source_target_pairs={{0,4},{4,8},{8,12},{12,16},{16,20},{20,24},{24,28},{1,5},{5,9},{9,... | collective-permute-start | bytes 1572872 | tf_op jit(solution)/shard_map/ppermute | solution.py:16
  17.8 1.9 collective-permute-start.1
  19.8 0.0 collective-permute-done.4
  19.8 0.0 collective-permute-done.3
  19.8 0.0 collective-permute-done.2
  19.8 0.1 collective-permute-start.5
  19.9 5.5 %shard_map.91 = (s32[27,8192]{1,0:T(8,128)}, s32[27,8192]{1,0:T(8,128)}) custom-call(s32[27,8192]{1,0:T(8,128)} %bitcast.14), custom_call_target="tpu_custom_call" | custom-call | bytes 44236800 | tf_op jit(solution)/shard_map/pallas_call | solution.py:226
  25.4 0.1 pad_add_fusion.place_ref
  25.5 0.0 collective-permute-done.5.passed_ref
  25.5 0.0 collective-permute-done.low_ref
  25.5 5.7 %collective-permute-done.1.up_ref = bf16[2048,128]{1,0:T(8,128)(2,1)S(1)} collective-permute-done((bf16[2048,128]{1,0:T(8,128)(2,1)S(1)}, bf16[2048,128]{1,0:T(8,128)(2,1)S(1)}, u32[]{:S(2)}, u32[]{:S(2)}) %collective-permute-start.1) | collective-permute-done | bytes 524320 | tf_op jit(solution)/shard_map/ppermute | solution.py:16
  31.2 0.0 copy-done.1
  31.2 0.0 copy-done.9
  31.2 0.0 copy-done.8
  31.2 0.0 copy-start.6
  31.2 1.2 copy-done.6
  32.4 0.0 copy-start.7
  32.4 1.2 copy-done.7
  33.7 0.0 copy-start.2
  33.7 0.0 copy-start.3
  33.7 153.9 %shard_map.93.rows_ref = bf16[8192,128]{1,0:T(8,128)(2,1)S(1)} custom-call(s32[27,8192]{1,0:T(8,128)S(1)} %copy-done.6, s32[27,8192]{1,0:T(8,128)S(1)} %copy-done.6, s32[27,8192]{1,0:T(8,128)S(1)} %copy-done.7, bf16[8192,128]{1,0:T(8,128)(2,1)} %feat_ref.3, bf16[2048,128]{1,0:T(8,128)(2,1)S(1)} %collective-permute-done.low_ref, ...), custom_call_target="tpu_custom_call" | custom-call | flops 7247757312 | bytes 8388608 | tf_op jit(solution)/shard_map/pallas_call | solution.py:246
  187.6 0.0 copy-done.2
  187.6 0.0 copy-done.3
  187.6 50.6 %shard_map.94 = bf16[8192,128]{1,0:T(8,128)(2,1)S(1)} custom-call(s32[12288]{0:T(1024)S(1)} %copy-done.2, s32[8192]{0:T(1024)S(1)} %copy-done.3, bf16[8192,128]{1,0:T(8,128)(2,1)S(1)} %shard_map.93.rows_ref), custom_call_target="tpu_custom_call" | custom-call | tf_op jit(solution)/shard_map/pallas_call | solution.py:410
  238.2 1.3 copy.11
  (1 shorter events, 0.0 us)
Async XLA Ops:
  0.0 31.2 %copy-start.1 = (bf16[27,128,32]{1,2,0:T(8,128)(2,1)S(1)}, bf16[27,128,32]{1,2,0:T(8,128)(2,1)}, u32[]{:S(2)}) copy-start(bf16[27,128,32]{1,2,0:T(8,128)(2,1)} %param.15) | copy-start | bytes 663556
  0.0 31.2 %copy-start.9 = (f32[128]{0:T(128)S(1)}, f32[128]{0:T(128)}, u32[]{:S(2)}) copy-start(f32[128]{0:T(128)} %param.17) | copy-start | bytes 1540
  0.0 31.2 %copy-start.8 = (f32[128]{0:T(128)S(1)}, f32[128]{0:T(128)}, u32[]{:S(2)}) copy-start(f32[128]{0:T(128)} %param.16) | copy-start | bytes 1540
  1.0 18.8 %collective-permute-start.4 = (bf16[27,16,128]{2,1,0:T(8,128)(2,1)S(1)}, bf16[27,16,128]{2,1,0:T(8,128)(2,1)S(1)}, u32[]{:S(2)}, u32[]{:S(2)}) collective-permute-start(bf16[27,16,128]{2,1,0:T(8,128)(2,1)S(1)} %dynamic-slice_bitcast_fusion), channel_id=1, source_target_pairs={{0,3},{1,0},{2,1},{3,2},{4,7},{5,4},{6,5},{7,6},{8,11},{9,8},{10,9... | collective-permute-start | bytes 331784 | tf_op jit(solution)/shard_map/ppermute | solution.py:436
  5.1 14.6 %collective-permute-start.3 = (bf16[27,16,128]{2,1,0:T(8,128)(2,1)S(1)}, bf16[27,16,128]{2,1,0:T(8,128)(2,1)S(1)}, u32[]{:S(2)}, u32[]{:S(2)}) collective-permute-start(bf16[27,16,128]{2,1,0:T(8,128)(2,1)S(1)} %dynamic-slice_bitcast_fusion), channel_id=1, source_target_pairs={{0,2},{1,3},{2,0},{3,1},{4,6},{5,7},{6,4},{7,5},{8,10},{9,11},{10,... | collective-permute-start | bytes 331784 | tf_op jit(solution)/shard_map/ppermute | solution.py:436
  5.1 14.6 %collective-permute-start.2 = (bf16[27,16,128]{2,1,0:T(8,128)(2,1)S(1)}, bf16[27,16,128]{2,1,0:T(8,128)(2,1)S(1)}, u32[]{:S(2)}, u32[]{:S(2)}) collective-permute-start(bf16[27,16,128]{2,1,0:T(8,128)(2,1)S(1)} %dynamic-slice_bitcast_fusion), channel_id=1, source_target_pairs={{0,1},{1,2},{2,3},{3,0},{4,5},{5,6},{6,7},{7,4},{8,9},{9,10},{10,1... | collective-permute-start | bytes 331784 | tf_op jit(solution)/shard_map/ppermute | solution.py:436
  5.6 1.6 copy-start
  7.2 0.7 copy-start.4
  7.9 0.7 copy-start.5
  13.3 12.2 %collective-permute-start = (bf16[2048,128]{1,0:T(8,128)(2,1)S(1)}, bf16[2048,128]{1,0:T(8,128)(2,1)S(1)}, u32[]{:S(2)}, u32[]{:S(2)}) collective-permute-start(bf16[2048,128]{1,0:T(8,128)(2,1)S(1)} %get-tuple-element.11), channel_id=1, source_target_pairs={{0,4},{4,8},{8,12},{12,16},{16,20},{20,24},{24,28},{1,5},{5,9},{9,... | collective-permute-start | bytes 1572872 | tf_op jit(solution)/shard_map/ppermute | solution.py:16
  17.8 13.4 %collective-permute-start.1 = (bf16[2048,128]{1,0:T(8,128)(2,1)S(1)}, bf16[2048,128]{1,0:T(8,128)(2,1)S(1)}, u32[]{:S(2)}, u32[]{:S(2)}) collective-permute-start(bf16[2048,128]{1,0:T(8,128)(2,1)S(1)} %get-tuple-element.12), channel_id=1, source_target_pairs={{4,0},{8,4},{12,8},{16,12},{20,16},{24,20},{28,24},{5,1},{9,5},{13... | collective-permute-start | bytes 1572872 | tf_op jit(solution)/shard_map/ppermute | solution.py:16
  19.8 5.6 %collective-permute-start.5 = (bf16[3,27,16,128]{3,2,1,0:T(8,128)(2,1)S(1)}, bf16[3,27,16,128]{3,2,1,0:T(8,128)(2,1)S(1)}, u32[]{:S(2)}, u32[]{:S(2)}) collective-permute-start(bf16[3,27,16,128]{3,2,1,0:T(8,128)(2,1)S(1)} %pad_maximum_fusion.got_ref), channel_id=1, source_target_pairs={{0,4},{4,0},{8,12},{12,8},{16,20},{20,16},{24,28},{28,24},{1,5},{5... | collective-permute-start | bytes 995336 | tf_op jit(solution)/shard_map/ppermute | solution.py:440
  31.2 1.2 copy-start.6
  32.4 1.2 copy-start.7
  33.7 153.9 %copy-start.2 = (s32[12288]{0:T(1024)S(1)}, s32[12288]{0:T(1024)}, u32[]{:S(2)}) copy-start(s32[12288]{0:T(1024)} %send_ref.1) | copy-start | bytes 147460
  33.7 154.0 %copy-start.3 = (s32[8192]{0:T(1024)S(1)}, s32[8192]{0:T(1024)}, u32[]{:S(2)}) copy-start(s32[8192]{0:T(1024)} %recv_ref.1) | copy-start | bytes 98308

commit v7 on v6

--- a/solution.py
+++ b/solution.py
@@ -97,9 +97,12 @@
     tab_ref,
     buf_a,
     buf_b,
+    buf_c,
     acc_ref,
+    done_ref,
 ):
     step = pl.program_id(0)
+    steps = pl.num_programs(0) - 1
     rows, channels = feat_ref.shape
     halo = low_ref.shape[0]
     offsets, block = list_ref.shape
@@ -165,57 +168,73 @@
         result = jnp.dot(both, spread, preferred_element_type=jnp.float32)
         acc_ref[...] += result[:channels] + result[channels:]
 
-    own = feat_ref[pl.ds(pl.multiple_of(step * block, block), block), :]
+    def own_rows(at):
+        return feat_ref[pl.ds(pl.multiple_of(at * block, block), block), :]
+
+    def finish(at):
+        summed = done_ref[...]
+        centered = summed - jnp.mean(summed, axis=0, keepdims=True)
+        spread_sq = jnp.mean(centered * centered, axis=0, keepdims=True)
+        normed = centered * lax.rsqrt(spread_sq + 1e-05) * gain_ref[...] + shift_ref[...]
+        active = normed / (1.0 + jnp.exp(-normed))
+        blended = own_rows(at).astype(jnp.float32) + active.T
+        out_ref[...] = blended.astype(jnp.bfloat16)
+
     pairs = middle
 
     @pl.when(step == 0)
     def _():
-        gather(0, buf_a, count=1)
-
-    acc_ref[...] = lax.dot_general(
-        w_ref[middle], own, (((1,), (1,)), ((), ())), preferred_element_type=jnp.float32
-    )
-    gather(1, buf_b)
-    multiply(0, buf_a, count=1)
-
-    @pl.loop(0, (pairs - 3) // 4)
-    def _(p):
-        first = 1 + 4 * p
-        gather(first + 2, buf_a)
-        multiply(first, buf_b)
-        gather(first + 4, buf_b)
-        multiply(first + 2, buf_a)
-
-    gather(pairs - 2, buf_a)
-    multiply(pairs - 4, buf_b)
-
-    crowded = jnp.int32(0)
-    for k in range(offsets):
-        if k != middle:
-            crowded = crowded + jnp.where(list_ref[k, half] != absent, 1, 0)
-
-    @pl.when(crowded > 0)
+        gather(0, buf_a)
+
+    @pl.when(step < steps)
     def _():
-
-        @pl.loop(0, pairs)
+        gather(2, buf_b)
+        finish(jnp.maximum(step - 1, 0))
+        acc_ref[...] = lax.dot_general(
+            w_ref[middle],
+            own_rows(step),
+            (((1,), (1,)), ((), ())),
+            preferred_element_type=jnp.float32,
+        )
+        multiply(0, buf_a)
+
+        @pl.loop(0, (pairs - 5) // 4)
         def _(p):
-            more = (list_ref[offset_of(p, 0), half] != absent) | (
-                list_ref[offset_of(p, 1), half] != absent
-            )
-
-            @pl.when(more)
-            def _():
-                gather(p, buf_b, half, 1)
-                multiply(p, buf_b, half, 1)
-
-    multiply(pairs - 2, buf_a)
-    gather(0, buf_a, count=1, lists=next_ref)
-    summed = acc_ref[...].T
-    centered = summed - jnp.mean(summed, axis=-1, keepdims=True)
-    spread_sq = jnp.mean(centered * centered, axis=-1, keepdims=True)
-    normed = centered * lax.rsqrt(spread_sq + 1e-05) * gain_ref[...] + shift_ref[...]
-    blended = own.astype(jnp.float32) + normed / (1.0 + jnp.exp(-normed))
-    out_ref[...] = blended.astype(jnp.bfloat16)
+            first = 4 * p + 2
+            gather(first + 2, buf_a)
+            multiply(first, buf_b)
+            gather(first + 4, buf_b)
+            multiply(first + 2, buf_a)
+
+        gather(pairs - 1, buf_c, count=1)
+        multiply(pairs - 3, buf_b)
+
+        crowded = jnp.int32(0)
+        for k in range(offsets):
+            if k != middle:
+                crowded = crowded + jnp.where(list_ref[k, half] != absent, 1, 0)
+
+        @pl.when(crowded > 0)
+        def _():
+
+            @pl.loop(0, pairs)
+            def _(p):
+                more = (list_ref[offset_of(p, 0), half] != absent) | (
+                    list_ref[offset_of(p, 1), half] != absent
+                )
+
+                @pl.when(more)
+                def _():
+                    gather(p, buf_b, half, 1)
+                    multiply(p, buf_b, half, 1)
+
+        gather(0, buf_a, lists=next_ref)
+        multiply(pairs - 1, buf_c, count=1)
+        done_ref[...] = acc_ref[...]
+
+    @pl.when(step == steps)
+    def _():
+        finish(steps - 1)
 
 
 def compact(columns, absent):
@@ -245,14 +264,16 @@
     last = rows // block - 1
     return pl.pallas_call(
         conv_kernel,
-        grid=(rows // block,),
+        grid=(rows // block + 1,),
         out_shape=jax.ShapeDtypeStruct((rows, channels), jnp.bfloat16),
         in_specs=[
-            pl.BlockSpec((offsets, block), lambda i: (0, i), memory_space=pltpu.SMEM),
+            pl.BlockSpec(
+                (offsets, block), lambda i: (0, jnp.minimum(i, last)), memory_space=pltpu.SMEM
+            ),
             pl.BlockSpec(
                 (offsets, block), lambda i: (0, jnp.minimum(i + 1, last)), memory_space=pltpu.SMEM
             ),
-            pl.BlockSpec((offsets, block), lambda i: (0, i)),
+            pl.BlockSpec((offsets, block), lambda i: (0, jnp.minimum(i, last))),
             whole,
             whole,
             whole,
@@ -263,12 +284,14 @@
             whole,
             whole,
         ],
-        out_specs=pl.BlockSpec((block, channels), lambda i: (i, 0)),
+        out_specs=pl.BlockSpec((block, channels), lambda i: (jnp.maximum(i - 1, 0), 0)),
         scratch_shapes=[
             pltpu.VMEM((offsets, channels, channels), jnp.bfloat16),
             pltpu.VMEM((rows + 2 * halo + 8, channels), jnp.float32),
             pltpu.VMEM((2 * block, channels), jnp.float32),
             pltpu.VMEM((2 * block, channels), jnp.float32),
+            pltpu.VMEM((block, channels), jnp.float32),
+            pltpu.VMEM((channels, block), jnp.float32),
             pltpu.VMEM((channels, block), jnp.float32),
         ],
         compiler_params=pltpu.CompilerParams(vmem_limit_bytes=48 * 1024 * 1024),
@@ -458,8 +481,8 @@
         lists,
         places,
         weights,
-        norm_gain.reshape(1, channels),
-        norm_shift.reshape(1, channels),
+        jnp.broadcast_to(norm_gain[:, None], (channels, BLOCK)),
+        jnp.broadcast_to(norm_shift[:, None], (channels, BLOCK)),
     )
     return relay(blended, send_slot, recv_slot, "brick")
 

time: 241 us -> 245 us (1.017)
    unnamed x21 -> x23, local copies, waits for them, and re-layouts: 6.77 us -> 8.35 us
where the time goes in v7:
time: 245 us; the launch traced here: 244 us
  Pallas kernels  217 us (89%)
  starting transfers between devices  11.1 us (5%)
  local copies, waits for them, and re-layouts  9.48 us (4%)
  waiting for transfers between devices  5.72 us (2%)
    pallas_call x1, Pallas kernels, conv_block(): pl.pallas_call(conv_kernel, grid=(rows // block + 1,), out_shape=jax.Shap...  156 us
    pallas_call x1, Pallas kernels, relay(): pl.pallas_call(functools.partial(relay_kernel, axis=axis, count=count), o...  51.4 us
    unnamed x23, local copies, waits for them, and re-layouts  8.35 us
    ppermute x2, starting transfers between devices, shifted(): return lax.ppermute(block, axis, route)  6.44 us
    ppermute x2, waiting for transfers between devices, shifted(): return lax.ppermute(block, axis, route)  5.71 us
    pallas_call x1, Pallas kernels, compact(): pl.pallas_call(functools.partial(compact_kernel, absent=absent, block=BLO...  5.49 us
  transfers between devices with their start and end apart: 6, of which 1 were waited for; matrix products, arithmetic and copies ran while one was open for 0% of the time, Pallas kernels for 4%

profile of v7, /device:TPU:1, one launch (start us, length us, event | category | flops | bytes accessed | tf_op | source)
XLA Modules:
  0.0 244.0 jit_solution(17209745094161106324)
XLA Ops:
  0.0 0.0 copy-start.9
  0.0 0.0 copy-start.10
  0.0 0.0 copy-start.2
  0.0 1.0 dynamic-slice_bitcast_fusion
  1.0 4.2 %collective-permute-start.4 = (bf16[27,16,128]{2,1,0:T(8,128)(2,1)S(1)}, bf16[27,16,128]{2,1,0:T(8,128)(2,1)S(1)}, u32[]{:S(2)}, u32[]{:S(2)}) collective-permute-start(bf16[27,16,128]{2,1,0:T(8,128)(2,1)S(1)} %dynamic-slice_bitcast_fusion), channel_id=1, source_target_pairs={{0,3},{1,0},{2,1},{3,2},{4,7},{5,4},{6,5},{7,6},{8,11},{9,8},{10,9... | collective-permute-start | bytes 331784 | tf_op jit(solution)/shard_map/ppermute | solution.py:459
  5.1 0.0 collective-permute-start.3
  5.1 0.5 collective-permute-start.2
  5.6 0.0 copy-start
  5.6 1.6 copy-done
  7.2 0.0 copy-start.5
  7.2 0.7 copy-done.5
  7.9 0.0 copy-start.6
  7.9 0.7 copy-done.6
  8.6 4.7 %shard_map.92 = (bf16[2048,128]{1,0:T(8,128)(2,1)S(1)}, bf16[2048,128]{1,0:T(8,128)(2,1)S(1)}) custom-call(s32[2048]{0:T(1024)S(1)} %copy-done.5, s32[2048]{0:T(1024)S(1)} %copy-done.6, bf16[8192,128]{1,0:T(8,128)(2,1)S(1)} %copy-done), custom_call_target="tpu_custom_call" | custom-call | tf_op jit(solution)/shard_map/pallas_call | solution.py:46
  13.3 4.5 %collective-permute-start = (bf16[2048,128]{1,0:T(8,128)(2,1)S(1)}, bf16[2048,128]{1,0:T(8,128)(2,1)S(1)}, u32[]{:S(2)}, u32[]{:S(2)}) collective-permute-start(bf16[2048,128]{1,0:T(8,128)(2,1)S(1)} %get-tuple-element.11), channel_id=1, source_target_pairs={{0,4},{4,8},{8,12},{12,16},{16,20},{20,24},{24,28},{1,5},{5,9},{9,... | collective-permute-start | bytes 1572872 | tf_op jit(solution)/shard_map/ppermute | solution.py:16
  17.8 1.9 collective-permute-start.1
  19.8 0.0 collective-permute-done.4
  19.8 0.0 collective-permute-done.3
  19.8 0.0 collective-permute-done.2
  19.8 0.1 collective-permute-start.5
  19.9 5.5 %shard_map.91 = (s32[27,8192]{1,0:T(8,128)}, s32[27,8192]{1,0:T(8,128)}) custom-call(s32[27,8192]{1,0:T(8,128)} %bitcast.10), custom_call_target="tpu_custom_call" | custom-call | bytes 44236800 | tf_op jit(solution)/shard_map/pallas_call | solution.py:245
  25.4 0.1 pad_add_fusion.place_ref
  25.5 0.0 collective-permute-done.5.passed_ref
  25.5 0.0 collective-permute-done.low_ref
  25.5 5.7 %collective-permute-done.1.up_ref = bf16[2048,128]{1,0:T(8,128)(2,1)S(1)} collective-permute-done((bf16[2048,128]{1,0:T(8,128)(2,1)S(1)}, bf16[2048,128]{1,0:T(8,128)(2,1)S(1)}, u32[]{:S(2)}, u32[]{:S(2)}) %collective-permute-start.1) | collective-permute-done | bytes 524320 | tf_op jit(solution)/shard_map/ppermute | solution.py:16
  31.2 0.0 copy-done.9
  31.2 0.1 broadcast_in_dim.4.gain_ref
  31.3 0.0 copy-done.10
  31.3 0.1 broadcast_in_dim.5.shift_ref
  31.4 0.0 copy-done.2
  31.4 0.0 copy-start.7
  31.4 1.2 copy-done.7
  32.6 0.0 copy-start.8
  32.6 1.2 copy-done.8
  33.8 0.0 copy-start.3
  33.8 0.0 copy-start.4
  33.9 155.8 %shard_map.93.rows_ref = bf16[8192,128]{1,0:T(8,128)(2,1)} custom-call(s32[27,8192]{1,0:T(8,128)S(1)} %copy-done.7, s32[27,8192]{1,0:T(8,128)S(1)} %copy-done.7, s32[27,8192]{1,0:T(8,128)S(1)} %copy-done.8, bf16[8192,128]{1,0:T(8,128)(2,1)} %feat_ref.3, bf16[2048,128]{1,0:T(8,128)(2,1)S(1)} %collective-permute-done.low_ref, ...), custom_call_target="tpu_custom_call" | custom-call | flops 7247757312 | bytes 8388608 | tf_op jit(solution)/shard_map/pallas_call | solution.py:265
  189.7 0.0 copy-done.3
  189.7 0.0 copy-done.4
  189.7 0.0 copy-start.1
  189.7 1.6 copy-done.1
  191.3 51.4 %shard_map.94 = bf16[8192,128]{1,0:T(8,128)(2,1)S(1)} custom-call(s32[12288]{0:T(1024)S(1)} %copy-done.3, s32[8192]{0:T(1024)S(1)} %copy-done.4, bf16[8192,128]{1,0:T(8,128)(2,1)S(1)} %copy-done.1), custom_call_target="tpu_custom_call" | custom-call | tf_op jit(solution)/shard_map/pallas_call | solution.py:433
  242.7 1.3 copy.11
  (1 shorter events, 0.0 us)
Async XLA Ops:
  0.0 31.2 %copy-start.9 = (f32[128]{0:T(128)S(1)}, f32[128]{0:T(128)}, u32[]{:S(2)}) copy-start(f32[128]{0:T(128)} %param.16) | copy-start | bytes 1540
  0.0 31.3 %copy-start.10 = (f32[128]{0:T(128)S(1)}, f32[128]{0:T(128)}, u32[]{:S(2)}) copy-start(f32[128]{0:T(128)} %param.17) | copy-start | bytes 1540
  0.0 31.4 %copy-start.2 = (bf16[27,128,32]{1,2,0:T(8,128)(2,1)S(1)}, bf16[27,128,32]{1,2,0:T(8,128)(2,1)}, u32[]{:S(2)}) copy-start(bf16[27,128,32]{1,2,0:T(8,128)(2,1)} %param.15) | copy-start | bytes 663556
  1.0 18.8 %collective-permute-start.4 = (bf16[27,16,128]{2,1,0:T(8,128)(2,1)S(1)}, bf16[27,16,128]{2,1,0:T(8,128)(2,1)S(1)}, u32[]{:S(2)}, u32[]{:S(2)}) collective-permute-start(bf16[27,16,128]{2,1,0:T(8,128)(2,1)S(1)} %dynamic-slice_bitcast_fusion), channel_id=1, source_target_pairs={{0,3},{1,0},{2,1},{3,2},{4,7},{5,4},{6,5},{7,6},{8,11},{9,8},{10,9... | collective-permute-start | bytes 331784 | tf_op jit(solution)/shard_map/ppermute | solution.py:459
  5.1 14.6 %collective-permute-start.3 = (bf16[27,16,128]{2,1,0:T(8,128)(2,1)S(1)}, bf16[27,16,128]{2,1,0:T(8,128)(2,1)S(1)}, u32[]{:S(2)}, u32[]{:S(2)}) collective-permute-start(bf16[27,16,128]{2,1,0:T(8,128)(2,1)S(1)} %dynamic-slice_bitcast_fusion), channel_id=1, source_target_pairs={{0,2},{1,3},{2,0},{3,1},{4,6},{5,7},{6,4},{7,5},{8,10},{9,11},{10,... | collective-permute-start | bytes 331784 | tf_op jit(solution)/shard_map/ppermute | solution.py:459
  5.1 14.6 %collective-permute-start.2 = (bf16[27,16,128]{2,1,0:T(8,128)(2,1)S(1)}, bf16[27,16,128]{2,1,0:T(8,128)(2,1)S(1)}, u32[]{:S(2)}, u32[]{:S(2)}) collective-permute-start(bf16[27,16,128]{2,1,0:T(8,128)(2,1)S(1)} %dynamic-slice_bitcast_fusion), channel_id=1, source_target_pairs={{0,1},{1,2},{2,3},{3,0},{4,5},{5,6},{6,7},{7,4},{8,9},{9,10},{10,1... | collective-permute-start | bytes 331784 | tf_op jit(solution)/shard_map/ppermute | solution.py:459
  5.6 1.6 copy-start
  7.2 0.7 copy-start.5
  7.9 0.7 copy-start.6
  13.3 12.2 %collective-permute-start = (bf16[2048,128]{1,0:T(8,128)(2,1)S(1)}, bf16[2048,128]{1,0:T(8,128)(2,1)S(1)}, u32[]{:S(2)}, u32[]{:S(2)}) collective-permute-start(bf16[2048,128]{1,0:T(8,128)(2,1)S(1)} %get-tuple-element.11), channel_id=1, source_target_pairs={{0,4},{4,8},{8,12},{12,16},{16,20},{20,24},{24,28},{1,5},{5,9},{9,... | collective-permute-start | bytes 1572872 | tf_op jit(solution)/shard_map/ppermute | solution.py:16
  17.8 13.4 %collective-permute-start.1 = (bf16[2048,128]{1,0:T(8,128)(2,1)S(1)}, bf16[2048,128]{1,0:T(8,128)(2,1)S(1)}, u32[]{:S(2)}, u32[]{:S(2)}) collective-permute-start(bf16[2048,128]{1,0:T(8,128)(2,1)S(1)} %get-tuple-element.12), channel_id=1, source_target_pairs={{4,0},{8,4},{12,8},{16,12},{20,16},{24,20},{28,24},{5,1},{9,5},{13... | collective-permute-start | bytes 1572872 | tf_op jit(solution)/shard_map/ppermute | solution.py:16
  19.8 5.6 %collective-permute-start.5 = (bf16[3,27,16,128]{3,2,1,0:T(8,128)(2,1)S(1)}, bf16[3,27,16,128]{3,2,1,0:T(8,128)(2,1)S(1)}, u32[]{:S(2)}, u32[]{:S(2)}) collective-permute-start(bf16[3,27,16,128]{3,2,1,0:T(8,128)(2,1)S(1)} %pad_maximum_fusion.got_ref), channel_id=1, source_target_pairs={{0,4},{4,0},{8,12},{12,8},{16,20},{20,16},{24,28},{28,24},{1,5},{5... | collective-permute-start | bytes 995336 | tf_op jit(solution)/shard_map/ppermute | solution.py:463
  31.4 1.2 copy-start.7
  32.6 1.2 copy-start.8
  33.8 155.8 %copy-start.3 = (s32[12288]{0:T(1024)S(1)}, s32[12288]{0:T(1024)}, u32[]{:S(2)}) copy-start(s32[12288]{0:T(1024)} %send_ref.1) | copy-start | bytes 147460
  33.8 155.8 %copy-start.4 = (s32[8192]{0:T(1024)S(1)}, s32[8192]{0:T(1024)}, u32[]{:S(2)}) copy-start(s32[8192]{0:T(1024)} %recv_ref.1) | copy-start | bytes 98308
  189.7 1.6 copy-start.1

commit v8 on v7

--- a/solution.py
+++ b/solution.py
@@ -76,7 +76,13 @@
         moves = (word & (16384 << bit)) != 0
         moved = pltpu.roll(jnp.where(moves, word, 0), width - (1 << bit), 1)
         word = jnp.where(moves, 0, word) + moved
-    list_ref[...] = jnp.where(word != 0, word & 16383, absent)
+    listed = jnp.where(word != 0, word & 16383, absent)
+    half = list_ref.shape[2]
+    stride = list_ref.shape[1] // 2
+    for i in range(list_ref.shape[0]):
+        for h in range(2):
+            at = i * block + h * half
+            list_ref[i, h * stride : h * stride + offsets, :] = listed[:, at : at + half]
 
 
 def conv_kernel(
@@ -105,8 +111,9 @@
     steps = pl.num_programs(0) - 1
     rows, channels = feat_ref.shape
     halo = low_ref.shape[0]
-    offsets, block = list_ref.shape
+    offsets, block = pos_ref.shape
     half = block // 2
+    second = list_ref.shape[0] // 2
     middle = offsets // 2
     absent = rows + 2 * halo
     table = tab_ref.reshape(tab_ref.shape[0], 1, channels)
@@ -145,8 +152,9 @@
     def gather(pair, buf, base=0, count=2, lists=list_ref):
         for j in range(2 * count):
             k = offset_of(pair, j)
+            first = k * half + (second if base else 0)
             for c in range(half):
-                buf[pl.ds(j * half + c, 1), :] = table[lists[k, base + c]]
+                buf[pl.ds(j * half + c, 1), :] = table[lists[first + c]]
 
     def multiply(pair, buf, base=0, count=2):
         products, spreads = [], []
@@ -212,15 +220,15 @@
         crowded = jnp.int32(0)
         for k in range(offsets):
             if k != middle:
-                crowded = crowded + jnp.where(list_ref[k, half] != absent, 1, 0)
+                crowded = crowded + jnp.where(list_ref[second + k * half] != absent, 1, 0)
 
         @pl.when(crowded > 0)
         def _():
 
             @pl.loop(0, pairs)
             def _(p):
-                more = (list_ref[offset_of(p, 0), half] != absent) | (
-                    list_ref[offset_of(p, 1), half] != absent
+                more = (list_ref[second + offset_of(p, 0) * half] != absent) | (
+                    list_ref[second + offset_of(p, 1) * half] != absent
                 )
 
                 @pl.when(more)
@@ -240,26 +248,32 @@
 def compact(columns, absent):
     offsets, rows = columns.shape
     width = 8 * BLOCK
+    stride = -(-offsets // 8) * 8
+    lists = (width // BLOCK, 2 * stride, BLOCK // 2)
     spec = pl.BlockSpec((offsets, width), lambda i: (0, i))
-    shape = jax.ShapeDtypeStruct((offsets, rows), jnp.int32)
-    return pl.pallas_call(
+    listed, places = pl.pallas_call(
         functools.partial(compact_kernel, absent=absent, block=BLOCK),
         grid=(rows // width,),
-        out_shape=(shape, shape),
+        out_shape=(
+            jax.ShapeDtypeStruct((rows // BLOCK, *lists[1:]), jnp.int32),
+            jax.ShapeDtypeStruct((offsets, rows), jnp.int32),
+        ),
         in_specs=[spec],
-        out_specs=(spec, spec),
+        out_specs=(pl.BlockSpec(lists, lambda i: (i, 0, 0)), spec),
         cost_estimate=pl.CostEstimate(
             flops=0, bytes_accessed=200 * rows * offsets, transcendentals=0
         ),
     )(columns)
+    return listed.reshape(-1), places
 
 
 def conv_block(features, from_lower, from_upper, lists, places, weights, gain, shift):
     place, mine, got, passed = weights
     rows, channels = features.shape
     halo = from_lower.shape[0]
-    offsets = lists.shape[0]
+    offsets = places.shape[0]
     block = BLOCK
+    span = lists.shape[0] // (rows // block)
     whole = pl.BlockSpec(memory_space=pltpu.VMEM)
     last = rows // block - 1
     return pl.pallas_call(
@@ -267,12 +281,8 @@
         grid=(rows // block + 1,),
         out_shape=jax.ShapeDtypeStruct((rows, channels), jnp.bfloat16),
         in_specs=[
-            pl.BlockSpec(
-                (offsets, block), lambda i: (0, jnp.minimum(i, last)), memory_space=pltpu.SMEM
-            ),
-            pl.BlockSpec(
-                (offsets, block), lambda i: (0, jnp.minimum(i + 1, last)), memory_space=pltpu.SMEM
-            ),
+            pl.BlockSpec((span,), lambda i: (jnp.minimum(i, last),), memory_space=pltpu.SMEM),
+            pl.BlockSpec((span,), lambda i: (jnp.minimum(i + 1, last),), memory_space=pltpu.SMEM),
             pl.BlockSpec((offsets, block), lambda i: (0, jnp.minimum(i, last))),
             whole,
             whole,

time: 245 us -> 229 us (0.935)
  Pallas kernels: 217 us -> 203 us
    pallas_call x1, Pallas kernels: 156 us -> 141 us  [conv_block(): pl.pallas_call(conv_kernel, grid=(rows // block + 1,), out_shape=jax.Shap...]
where the time goes in v8:
time: 229 us
  Pallas kernels  203 us (89%)
  starting transfers between devices  11.1 us (5%)
  local copies, waits for them, and re-layouts  9.48 us (4%)
  waiting for transfers between devices  5.72 us (2%)
    pallas_call x1, Pallas kernels, conv_block(): pl.pallas_call(conv_kernel, grid=(rows // block + 1,), out_shape=jax.Shap...  141 us
    pallas_call x1, Pallas kernels, relay(): pl.pallas_call(functools.partial(relay_kernel, axis=axis, count=count), o...  51.4 us
    unnamed x23, local copies, waits for them, and re-layouts  8.35 us
    ppermute x2, starting transfers between devices, shifted(): return lax.ppermute(block, axis, route)  6.44 us
    ppermute x2, waiting for transfers between devices, shifted(): return lax.ppermute(block, axis, route)  5.71 us
    pallas_call x1, Pallas kernels, compact(): pl.pallas_call(functools.partial(compact_kernel, absent=absent, block=BLO...  5.49 us
    pallas_call x1, Pallas kernels, pick_halo(): pl.pallas_call(pick_kernel, out_shape=(shape, shape), in_specs=[scalars,...  4.72 us
    ppermute x3, starting transfers between devices, spread_weights(): lax.ppermute(half, 'grp', [(i, (i + j) % groups) for i in range(groups)])  4.6 us
  transfers between devices with their start and end apart: 6, of which 1 were waited for; matrix products, arithmetic and copies ran while one was open for 0% of the time, Pallas kernels for 4%

profile of v8, /device:TPU:1, one launch (start us, length us, event | category | flops | bytes accessed | tf_op | source)
XLA Modules:
  0.0 229.1 jit_solution(1107342131976320667)
XLA Ops:
  0.0 0.0 copy-start.9
  0.0 0.0 copy-start.10
  0.0 0.0 copy-start.2
  0.0 1.0 dynamic-slice_bitcast_fusion
  1.0 4.2 %collective-permute-start.4 = (bf16[27,16,128]{2,1,0:T(8,128)(2,1)S(1)}, bf16[27,16,128]{2,1,0:T(8,128)(2,1)S(1)}, u32[]{:S(2)}, u32[]{:S(2)}) collective-permute-start(bf16[27,16,128]{2,1,0:T(8,128)(2,1)S(1)} %dynamic-slice_bitcast_fusion), channel_id=1, source_target_pairs={{0,3},{1,0},{2,1},{3,2},{4,7},{5,4},{6,5},{7,6},{8,11},{9,8},{10,9... | collective-permute-start | bytes 331784 | tf_op jit(solution)/shard_map/ppermute | solution.py:469
  5.1 0.0 collective-permute-start.3
  5.1 0.5 collective-permute-start.2
  5.6 0.0 copy-start
  5.6 1.6 copy-done
  7.2 0.0 copy-start.5
  7.2 0.7 copy-done.5
  7.9 0.0 copy-start.6
  7.9 0.7 copy-done.6
  8.6 4.7 %shard_map.92 = (bf16[2048,128]{1,0:T(8,128)(2,1)S(1)}, bf16[2048,128]{1,0:T(8,128)(2,1)S(1)}) custom-call(s32[2048]{0:T(1024)S(1)} %copy-done.5, s32[2048]{0:T(1024)S(1)} %copy-done.6, bf16[8192,128]{1,0:T(8,128)(2,1)S(1)} %copy-done), custom_call_target="tpu_custom_call" | custom-call | tf_op jit(solution)/shard_map/pallas_call | solution.py:46
  13.3 4.5 %collective-permute-start = (bf16[2048,128]{1,0:T(8,128)(2,1)S(1)}, bf16[2048,128]{1,0:T(8,128)(2,1)S(1)}, u32[]{:S(2)}, u32[]{:S(2)}) collective-permute-start(bf16[2048,128]{1,0:T(8,128)(2,1)S(1)} %get-tuple-element.11), channel_id=1, source_target_pairs={{0,4},{4,8},{8,12},{12,16},{16,20},{20,24},{24,28},{1,5},{5,9},{9,... | collective-permute-start | bytes 1572872 | tf_op jit(solution)/shard_map/ppermute | solution.py:16
  17.8 1.9 collective-permute-start.1
  19.8 0.0 collective-permute-done.4
  19.8 0.0 collective-permute-done.3
  19.8 0.0 collective-permute-done.2
  19.8 0.1 collective-permute-start.5
  19.9 5.5 %shard_map.91 = (s32[32,64,128]{2,1,0:T(8,128)}, s32[27,8192]{1,0:T(8,128)}) custom-call(s32[27,8192]{1,0:T(8,128)} %bitcast.13), custom_call_target="tpu_custom_call" | custom-call | bytes 44236800 | tf_op jit(solution)/shard_map/pallas_call | solution.py:254
  25.4 0.1 pad_add_fusion.place_ref
  25.5 0.0 collective-permute-done.5.passed_ref
  25.5 0.0 collective-permute-done.low_ref
  25.5 5.7 %collective-permute-done.1.up_ref = bf16[2048,128]{1,0:T(8,128)(2,1)S(1)} collective-permute-done((bf16[2048,128]{1,0:T(8,128)(2,1)S(1)}, bf16[2048,128]{1,0:T(8,128)(2,1)S(1)}, u32[]{:S(2)}, u32[]{:S(2)}) %collective-permute-start.1) | collective-permute-done | bytes 524320 | tf_op jit(solution)/shard_map/ppermute | solution.py:16
  31.2 0.0 copy-done.9
  31.2 0.1 broadcast_in_dim.4.gain_ref
  31.3 0.0 copy-done.10
  31.3 0.1 broadcast_in_dim.5.shift_ref
  31.4 0.0 copy-done.2
  31.4 0.0 copy-start.7
  31.4 1.2 copy-done.7
  32.6 0.0 copy-start.8
  32.6 1.2 copy-done.8
  33.8 0.0 copy-start.3
  33.8 0.0 copy-start.4
  33.9 140.9 %shard_map.93.rows_ref = bf16[8192,128]{1,0:T(8,128)(2,1)} custom-call(s32[262144]{0:T(1024)S(1)} %bitcast.11, s32[262144]{0:T(1024)S(1)} %bitcast.12, s32[27,8192]{1,0:T(8,128)S(1)} %copy-done.8, bf16[8192,128]{1,0:T(8,128)(2,1)} %feat_ref.3, bf16[2048,128]{1,0:T(8,128)(2,1)S(1)} %collective-permute-done.low_ref, ...), custom_call_target="tpu_custom_call" | custom-call | flops 7247757312 | bytes 8388608 | tf_op jit(solution)/shard_map/pallas_call | solution.py:279
  174.7 0.0 copy-done.3
  174.7 0.0 copy-done.4
  174.7 0.0 copy-start.1
  174.7 1.6 copy-done.1
  176.3 51.4 %shard_map.94 = bf16[8192,128]{1,0:T(8,128)(2,1)S(1)} custom-call(s32[12288]{0:T(1024)S(1)} %copy-done.3, s32[8192]{0:T(1024)S(1)} %copy-done.4, bf16[8192,128]{1,0:T(8,128)(2,1)S(1)} %copy-done.1), custom_call_target="tpu_custom_call" | custom-call | tf_op jit(solution)/shard_map/pallas_call | solution.py:443
  227.8 1.3 copy.11
  (1 shorter events, 0.0 us)
Async XLA Ops:
  0.0 31.2 %copy-start.9 = (f32[128]{0:T(128)S(1)}, f32[128]{0:T(128)}, u32[]{:S(2)}) copy-start(f32[128]{0:T(128)} %param.16) | copy-start | bytes 1540
  0.0 31.3 %copy-start.10 = (f32[128]{0:T(128)S(1)}, f32[128]{0:T(128)}, u32[]{:S(2)}) copy-start(f32[128]{0:T(128)} %param.17) | copy-start | bytes 1540
  0.0 31.4 %copy-start.2 = (bf16[27,128,32]{1,2,0:T(8,128)(2,1)S(1)}, bf16[27,128,32]{1,2,0:T(8,128)(2,1)}, u32[]{:S(2)}) copy-start(bf16[27,128,32]{1,2,0:T(8,128)(2,1)} %param.15) | copy-start | bytes 663556
  1.0 18.8 %collective-permute-start.4 = (bf16[27,16,128]{2,1,0:T(8,128)(2,1)S(1)}, bf16[27,16,128]{2,1,0:T(8,128)(2,1)S(1)}, u32[]{:S(2)}, u32[]{:S(2)}) collective-permute-start(bf16[27,16,128]{2,1,0:T(8,128)(2,1)S(1)} %dynamic-slice_bitcast_fusion), channel_id=1, source_target_pairs={{0,3},{1,0},{2,1},{3,2},{4,7},{5,4},{6,5},{7,6},{8,11},{9,8},{10,9... | collective-permute-start | bytes 331784 | tf_op jit(solution)/shard_map/ppermute | solution.py:469
  5.1 14.6 %collective-permute-start.3 = (bf16[27,16,128]{2,1,0:T(8,128)(2,1)S(1)}, bf16[27,16,128]{2,1,0:T(8,128)(2,1)S(1)}, u32[]{:S(2)}, u32[]{:S(2)}) collective-permute-start(bf16[27,16,128]{2,1,0:T(8,128)(2,1)S(1)} %dynamic-slice_bitcast_fusion), channel_id=1, source_target_pairs={{0,2},{1,3},{2,0},{3,1},{4,6},{5,7},{6,4},{7,5},{8,10},{9,11},{10,... | collective-permute-start | bytes 331784 | tf_op jit(solution)/shard_map/ppermute | solution.py:469
  5.1 14.6 %collective-permute-start.2 = (bf16[27,16,128]{2,1,0:T(8,128)(2,1)S(1)}, bf16[27,16,128]{2,1,0:T(8,128)(2,1)S(1)}, u32[]{:S(2)}, u32[]{:S(2)}) collective-permute-start(bf16[27,16,128]{2,1,0:T(8,128)(2,1)S(1)} %dynamic-slice_bitcast_fusion), channel_id=1, source_target_pairs={{0,1},{1,2},{2,3},{3,0},{4,5},{5,6},{6,7},{7,4},{8,9},{9,10},{10,1... | collective-permute-start | bytes 331784 | tf_op jit(solution)/shard_map/ppermute | solution.py:469
  5.6 1.6 copy-start
  7.2 0.7 copy-start.5
  7.9 0.7 copy-start.6
  13.3 12.2 %collective-permute-start = (bf16[2048,128]{1,0:T(8,128)(2,1)S(1)}, bf16[2048,128]{1,0:T(8,128)(2,1)S(1)}, u32[]{:S(2)}, u32[]{:S(2)}) collective-permute-start(bf16[2048,128]{1,0:T(8,128)(2,1)S(1)} %get-tuple-element.11), channel_id=1, source_target_pairs={{0,4},{4,8},{8,12},{12,16},{16,20},{20,24},{24,28},{1,5},{5,9},{9,... | collective-permute-start | bytes 1572872 | tf_op jit(solution)/shard_map/ppermute | solution.py:16
  17.8 13.4 %collective-permute-start.1 = (bf16[2048,128]{1,0:T(8,128)(2,1)S(1)}, bf16[2048,128]{1,0:T(8,128)(2,1)S(1)}, u32[]{:S(2)}, u32[]{:S(2)}) collective-permute-start(bf16[2048,128]{1,0:T(8,128)(2,1)S(1)} %get-tuple-element.12), channel_id=1, source_target_pairs={{4,0},{8,4},{12,8},{16,12},{20,16},{24,20},{28,24},{5,1},{9,5},{13... | collective-permute-start | bytes 1572872 | tf_op jit(solution)/shard_map/ppermute | solution.py:16
  19.8 5.6 %collective-permute-start.5 = (bf16[3,27,16,128]{3,2,1,0:T(8,128)(2,1)S(1)}, bf16[3,27,16,128]{3,2,1,0:T(8,128)(2,1)S(1)}, u32[]{:S(2)}, u32[]{:S(2)}) collective-permute-start(bf16[3,27,16,128]{3,2,1,0:T(8,128)(2,1)S(1)} %pad_maximum_fusion.got_ref), channel_id=1, source_target_pairs={{0,4},{4,0},{8,12},{12,8},{16,20},{20,16},{24,28},{28,24},{1,5},{5... | collective-permute-start | bytes 995336 | tf_op jit(solution)/shard_map/ppermute | solution.py:473
  31.4 1.2 copy-start.7
  32.6 1.2 copy-start.8
  33.8 140.9 %copy-start.3 = (s32[12288]{0:T(1024)S(1)}, s32[12288]{0:T(1024)}, u32[]{:S(2)}) copy-start(s32[12288]{0:T(1024)} %send_ref.1) | copy-start | bytes 147460
  33.8 140.9 %copy-start.4 = (s32[8192]{0:T(1024)S(1)}, s32[8192]{0:T(1024)}, u32[]{:S(2)}) copy-start(s32[8192]{0:T(1024)} %recv_ref.1) | copy-start | bytes 98308
  174.7 1.6 copy-start.1

commit v9 on v6

--- a/solution.py
+++ b/solution.py
@@ -76,7 +76,13 @@
         moves = (word & (16384 << bit)) != 0
         moved = pltpu.roll(jnp.where(moves, word, 0), width - (1 << bit), 1)
         word = jnp.where(moves, 0, word) + moved
-    list_ref[...] = jnp.where(word != 0, word & 16383, absent)
+    listed = jnp.where(word != 0, word & 16383, absent)
+    half = list_ref.shape[2]
+    stride = list_ref.shape[1] // 2
+    for i in range(list_ref.shape[0]):
+        for h in range(2):
+            at = i * block + h * half
+            list_ref[i, h * stride : h * stride + offsets, :] = listed[:, at : at + half]
 
 
 def conv_kernel(
@@ -102,8 +108,9 @@
     step = pl.program_id(0)
     rows, channels = feat_ref.shape
     halo = low_ref.shape[0]
-    offsets, block = list_ref.shape
+    offsets, block = pos_ref.shape
     half = block // 2
+    second = list_ref.shape[0] // 2
     middle = offsets // 2
     absent = rows + 2 * halo
     table = tab_ref.reshape(tab_ref.shape[0], 1, channels)
@@ -142,8 +149,9 @@
     def gather(pair, buf, base=0, count=2, lists=list_ref):
         for j in range(2 * count):
             k = offset_of(pair, j)
+            first = k * half + (second if base else 0)
             for c in range(half):
-                buf[pl.ds(j * half + c, 1), :] = table[lists[k, base + c]]
+                buf[pl.ds(j * half + c, 1), :] = table[lists[first + c]]
 
     def multiply(pair, buf, base=0, count=2):
         products, spreads = [], []
@@ -192,15 +200,15 @@
     crowded = jnp.int32(0)
     for k in range(offsets):
         if k != middle:
-            crowded = crowded + jnp.where(list_ref[k, half] != absent, 1, 0)
+            crowded = crowded + jnp.where(list_ref[second + k * half] != absent, 1, 0)
 
     @pl.when(crowded > 0)
     def _():
 
         @pl.loop(0, pairs)
         def _(p):
-            more = (list_ref[offset_of(p, 0), half] != absent) | (
-                list_ref[offset_of(p, 1), half] != absent
+            more = (list_ref[second + offset_of(p, 0) * half] != absent) | (
+                list_ref[second + offset_of(p, 1) * half] != absent
             )
 
             @pl.when(more)
@@ -221,26 +229,32 @@
 def compact(columns, absent):
     offsets, rows = columns.shape
     width = 8 * BLOCK
+    stride = -(-offsets // 8) * 8
+    lists = (width // BLOCK, 2 * stride, BLOCK // 2)
     spec = pl.BlockSpec((offsets, width), lambda i: (0, i))
-    shape = jax.ShapeDtypeStruct((offsets, rows), jnp.int32)
-    return pl.pallas_call(
+    listed, places = pl.pallas_call(
         functools.partial(compact_kernel, absent=absent, block=BLOCK),
         grid=(rows // width,),
-        out_shape=(shape, shape),
+        out_shape=(
+            jax.ShapeDtypeStruct((rows // BLOCK, *lists[1:]), jnp.int32),
+            jax.ShapeDtypeStruct((offsets, rows), jnp.int32),
+        ),
         in_specs=[spec],
-        out_specs=(spec, spec),
+        out_specs=(pl.BlockSpec(lists, lambda i: (i, 0, 0)), spec),
         cost_estimate=pl.CostEstimate(
             flops=0, bytes_accessed=200 * rows * offsets, transcendentals=0
         ),
     )(columns)
+    return listed.reshape(-1), places
 
 
 def conv_block(features, from_lower, from_upper, lists, places, weights, gain, shift):
     place, mine, got, passed = weights
     rows, channels = features.shape
     halo = from_lower.shape[0]
-    offsets = lists.shape[0]
+    offsets = places.shape[0]
     block = BLOCK
+    span = lists.shape[0] // (rows // block)
     whole = pl.BlockSpec(memory_space=pltpu.VMEM)
     last = rows // block - 1
     return pl.pallas_call(
@@ -248,10 +262,8 @@
         grid=(rows // block,),
         out_shape=jax.ShapeDtypeStruct((rows, channels), jnp.bfloat16),
         in_specs=[
-            pl.BlockSpec((offsets, block), lambda i: (0, i), memory_space=pltpu.SMEM),
-            pl.BlockSpec(
-                (offsets, block), lambda i: (0, jnp.minimum(i + 1, last)), memory_space=pltpu.SMEM
-            ),
+            pl.BlockSpec((span,), lambda i: (i,), memory_space=pltpu.SMEM),
+            pl.BlockSpec((span,), lambda i: (jnp.minimum(i + 1, last),), memory_space=pltpu.SMEM),
             pl.BlockSpec((offsets, block), lambda i: (0, i)),
             whole,
             whole,
@@ -335,8 +347,34 @@
     table_ref[pl.ds(rows, 8), :] = jnp.zeros((8, channels), jnp.float32)
     pl.semaphore_wait(barrier, count - 1)
 
+    bits = count.bit_length() - 1
+    axis_bits = (bits - 1) // 2
+    core = lax.rem(me, 2)
+
+    def exchanged(distance):
+        if bits != 2 * axis_bits + 1:
+            return distance
+        span = 1 << axis_bits
+        return distance % 2 + 2 * (distance // 2 % span * span + distance // 2 // span)
+
+    plane = sorted(range(2, count, 2), key=lambda d: -(exchanged(d) == d))
+    order = plane + [d + 1 for d in plane] + [1]
+
+    def distance_at(i):
+        d = jnp.int32(0)
+        for at, here in enumerate(order):
+            d = jnp.where(i == at, here + core * (exchanged(here) - here), d)
+        return d
+
+    def partner(distance):
+        at = jnp.int32(0)
+        for bit in range(bits):
+            scale = 1 << bit
+            at = at + scale * lax.rem(me // scale + distance // scale, 2)
+        return at
+
     def copy_to(j):
-        to = lax.rem(me + j, count)
+        to = partner(j)
         return pltpu.make_async_remote_copy(
             src_ref=outbox_ref.at[to],
             dst_ref=inbox_ref.at[me],
@@ -356,8 +394,9 @@
 
     @pl.loop(0, count - 1)
     def _(i):
-        j = lax.rem(i + count // 2, count - 1) + 1
-        fill(lax.rem(me + j, count), outbox_ref.at[lax.rem(me + j, count)])
+        j = distance_at(i)
+        to = partner(j)
+        fill(to, outbox_ref.at[to])
         copy_to(j).start()
 
     fill(me, inbox_ref.at[me])
@@ -375,8 +414,8 @@
 
     @pl.loop(0, count - 1)
     def _(i):
-        j = lax.rem(i + count // 2, count - 1) + 1
-        source = lax.rem(me - j + count, count)
+        j = distance_at(i)
+        source = partner(j)
         pltpu.make_async_remote_copy(
             src_ref=outbox_ref.at[source],
             dst_ref=inbox_ref.at[source],

time: 241 us -> 222 us (0.921)
  Pallas kernels: 215 us -> 196 us
    pallas_call x1, Pallas kernels: 154 us -> 137 us  [conv_block(): pl.pallas_call(conv_kernel, grid=(rows // block,), out_shape=jax.ShapeDty...]
  transfers between devices with their start and end apart: 6 -> 6, of which waited for: 1 -> 1; matrix products, arithmetic and copies ran while one was open for 0% -> 0% of each run, Pallas kernels for 4% -> 5%
where the time goes in v9:
time: 222 us; the launch traced here: 221 us
  Pallas kernels  196 us (88%)
  starting transfers between devices  11.1 us (5%)
  local copies, waits for them, and re-layouts  7.73 us (3%)
  waiting for transfers between devices  5.72 us (3%)
    pallas_call x1, Pallas kernels, conv_block(): pl.pallas_call(conv_kernel, grid=(rows // block,), out_shape=jax.ShapeDty...  137 us
    pallas_call x1, Pallas kernels, relay(): pl.pallas_call(functools.partial(relay_kernel, axis=axis, count=count), o...  48.9 us
    unnamed x21, local copies, waits for them, and re-layouts  6.77 us
    ppermute x2, starting transfers between devices, shifted(): return lax.ppermute(block, axis, route)  6.44 us
    ppermute x2, waiting for transfers between devices, shifted(): return lax.ppermute(block, axis, route)  5.71 us
    pallas_call x1, Pallas kernels, compact(): pl.pallas_call(functools.partial(compact_kernel, absent=absent, block=BLO...  5.49 us
    pallas_call x1, Pallas kernels, pick_halo(): pl.pallas_call(pick_kernel, out_shape=(shape, shape), in_specs=[scalars,...  4.72 us
    ppermute x3, starting transfers between devices, spread_weights(): lax.ppermute(half, 'grp', [(i, (i + j) % groups) for i in range(groups)])  4.6 us
  transfers between devices with their start and end apart: 6, of which 1 were waited for; matrix products, arithmetic and copies ran while one was open for 0% of the time, Pallas kernels for 5%

profile of v9, /device:TPU:1, one launch (start us, length us, event | category | flops | bytes accessed | tf_op | source)
XLA Modules:
  0.0 220.9 jit_solution(6416609119691558737)
XLA Ops:
  0.0 0.0 copy-start.1
  0.0 0.0 copy-start.9
  0.0 0.0 copy-start.8
  0.0 1.0 dynamic-slice_bitcast_fusion
  1.0 4.2 %collective-permute-start.4 = (bf16[27,16,128]{2,1,0:T(8,128)(2,1)S(1)}, bf16[27,16,128]{2,1,0:T(8,128)(2,1)S(1)}, u32[]{:S(2)}, u32[]{:S(2)}) collective-permute-start(bf16[27,16,128]{2,1,0:T(8,128)(2,1)S(1)} %dynamic-slice_bitcast_fusion), channel_id=1, source_target_pairs={{0,3},{1,0},{2,1},{3,2},{4,7},{5,4},{6,5},{7,6},{8,11},{9,8},{10,9... | collective-permute-start | bytes 331784 | tf_op jit(solution)/shard_map/ppermute | solution.py:475
  5.1 0.0 collective-permute-start.3
  5.1 0.5 collective-permute-start.2
  5.6 0.0 copy-start
  5.6 1.6 copy-done
  7.2 0.0 copy-start.4
  7.2 0.7 copy-done.4
  7.9 0.0 copy-start.5
  7.9 0.7 copy-done.5
  8.6 4.7 %shard_map.92 = (bf16[2048,128]{1,0:T(8,128)(2,1)S(1)}, bf16[2048,128]{1,0:T(8,128)(2,1)S(1)}) custom-call(s32[2048]{0:T(1024)S(1)} %copy-done.4, s32[2048]{0:T(1024)S(1)} %copy-done.5, bf16[8192,128]{1,0:T(8,128)(2,1)S(1)} %copy-done), custom_call_target="tpu_custom_call" | custom-call | tf_op jit(solution)/shard_map/pallas_call | solution.py:46
  13.3 4.5 %collective-permute-start = (bf16[2048,128]{1,0:T(8,128)(2,1)S(1)}, bf16[2048,128]{1,0:T(8,128)(2,1)S(1)}, u32[]{:S(2)}, u32[]{:S(2)}) collective-permute-start(bf16[2048,128]{1,0:T(8,128)(2,1)S(1)} %get-tuple-element.11), channel_id=1, source_target_pairs={{0,4},{4,8},{8,12},{12,16},{16,20},{20,24},{24,28},{1,5},{5,9},{9,... | collective-permute-start | bytes 1572872 | tf_op jit(solution)/shard_map/ppermute | solution.py:16
  17.8 1.9 collective-permute-start.1
  19.8 0.0 collective-permute-done.4
  19.8 0.0 collective-permute-done.3
  19.8 0.0 collective-permute-done.2
  19.8 0.1 collective-permute-start.5
  19.9 5.5 %shard_map.91 = (s32[32,64,128]{2,1,0:T(8,128)}, s32[27,8192]{1,0:T(8,128)}) custom-call(s32[27,8192]{1,0:T(8,128)} %bitcast.17), custom_call_target="tpu_custom_call" | custom-call | bytes 44236800 | tf_op jit(solution)/shard_map/pallas_call | solution.py:235
  25.4 0.1 pad_add_fusion.place_ref
  25.5 0.0 collective-permute-done.5.passed_ref
  25.5 0.0 collective-permute-done.low_ref
  25.5 5.7 %collective-permute-done.1.up_ref = bf16[2048,128]{1,0:T(8,128)(2,1)S(1)} collective-permute-done((bf16[2048,128]{1,0:T(8,128)(2,1)S(1)}, bf16[2048,128]{1,0:T(8,128)(2,1)S(1)}, u32[]{:S(2)}, u32[]{:S(2)}) %collective-permute-start.1) | collective-permute-done | bytes 524320 | tf_op jit(solution)/shard_map/ppermute | solution.py:16
  31.2 0.0 copy-done.1
  31.2 0.0 copy-done.9
  31.2 0.0 copy-done.8
  31.2 0.0 copy-start.6
  31.2 1.2 copy-done.6
  32.4 0.0 copy-start.7
  32.4 1.2 copy-done.7
  33.7 0.0 copy-start.2
  33.7 0.0 copy-start.3
  33.7 136.9 %shard_map.93.rows_ref = bf16[8192,128]{1,0:T(8,128)(2,1)S(1)} custom-call(s32[262144]{0:T(1024)S(1)} %bitcast.13, s32[262144]{0:T(1024)S(1)} %bitcast.14, s32[27,8192]{1,0:T(8,128)S(1)} %copy-done.7, bf16[8192,128]{1,0:T(8,128)(2,1)} %feat_ref.3, bf16[2048,128]{1,0:T(8,128)(2,1)S(1)} %collective-permute-done.low_ref, ...), custom_call_target="tpu_custom_call" | custom-call | flops 7247757312 | bytes 8388608 | tf_op jit(solution)/shard_map/pallas_call | solution.py:260
  170.6 0.0 copy-done.2
  170.6 0.0 copy-done.3
  170.6 48.9 %shard_map.94 = bf16[8192,128]{1,0:T(8,128)(2,1)S(1)} custom-call(s32[12288]{0:T(1024)S(1)} %copy-done.2, s32[8192]{0:T(1024)S(1)} %copy-done.3, bf16[8192,128]{1,0:T(8,128)(2,1)S(1)} %shard_map.93.rows_ref), custom_call_target="tpu_custom_call" | custom-call | tf_op jit(solution)/shard_map/pallas_call | solution.py:449
  219.5 1.3 copy.11
  (1 shorter events, 0.0 us)
Async XLA Ops:
  0.0 31.2 %copy-start.1 = (bf16[27,128,32]{1,2,0:T(8,128)(2,1)S(1)}, bf16[27,128,32]{1,2,0:T(8,128)(2,1)}, u32[]{:S(2)}) copy-start(bf16[27,128,32]{1,2,0:T(8,128)(2,1)} %param.15) | copy-start | bytes 663556
  0.0 31.2 %copy-start.9 = (f32[128]{0:T(128)S(1)}, f32[128]{0:T(128)}, u32[]{:S(2)}) copy-start(f32[128]{0:T(128)} %param.17) | copy-start | bytes 1540
  0.0 31.2 %copy-start.8 = (f32[128]{0:T(128)S(1)}, f32[128]{0:T(128)}, u32[]{:S(2)}) copy-start(f32[128]{0:T(128)} %param.16) | copy-start | bytes 1540
  1.0 18.8 %collective-permute-start.4 = (bf16[27,16,128]{2,1,0:T(8,128)(2,1)S(1)}, bf16[27,16,128]{2,1,0:T(8,128)(2,1)S(1)}, u32[]{:S(2)}, u32[]{:S(2)}) collective-permute-start(bf16[27,16,128]{2,1,0:T(8,128)(2,1)S(1)} %dynamic-slice_bitcast_fusion), channel_id=1, source_target_pairs={{0,3},{1,0},{2,1},{3,2},{4,7},{5,4},{6,5},{7,6},{8,11},{9,8},{10,9... | collective-permute-start | bytes 331784 | tf_op jit(solution)/shard_map/ppermute | solution.py:475
  5.1 14.6 %collective-permute-start.3 = (bf16[27,16,128]{2,1,0:T(8,128)(2,1)S(1)}, bf16[27,16,128]{2,1,0:T(8,128)(2,1)S(1)}, u32[]{:S(2)}, u32[]{:S(2)}) collective-permute-start(bf16[27,16,128]{2,1,0:T(8,128)(2,1)S(1)} %dynamic-slice_bitcast_fusion), channel_id=1, source_target_pairs={{0,2},{1,3},{2,0},{3,1},{4,6},{5,7},{6,4},{7,5},{8,10},{9,11},{10,... | collective-permute-start | bytes 331784 | tf_op jit(solution)/shard_map/ppermute | solution.py:475
  5.1 14.6 %collective-permute-start.2 = (bf16[27,16,128]{2,1,0:T(8,128)(2,1)S(1)}, bf16[27,16,128]{2,1,0:T(8,128)(2,1)S(1)}, u32[]{:S(2)}, u32[]{:S(2)}) collective-permute-start(bf16[27,16,128]{2,1,0:T(8,128)(2,1)S(1)} %dynamic-slice_bitcast_fusion), channel_id=1, source_target_pairs={{0,1},{1,2},{2,3},{3,0},{4,5},{5,6},{6,7},{7,4},{8,9},{9,10},{10,1... | collective-permute-start | bytes 331784 | tf_op jit(solution)/shard_map/ppermute | solution.py:475
  5.6 1.6 copy-start
  7.2 0.7 copy-start.4
  7.9 0.7 copy-start.5
  13.3 12.2 %collective-permute-start = (bf16[2048,128]{1,0:T(8,128)(2,1)S(1)}, bf16[2048,128]{1,0:T(8,128)(2,1)S(1)}, u32[]{:S(2)}, u32[]{:S(2)}) collective-permute-start(bf16[2048,128]{1,0:T(8,128)(2,1)S(1)} %get-tuple-element.11), channel_id=1, source_target_pairs={{0,4},{4,8},{8,12},{12,16},{16,20},{20,24},{24,28},{1,5},{5,9},{9,... | collective-permute-start | bytes 1572872 | tf_op jit(solution)/shard_map/ppermute | solution.py:16
  17.8 13.4 %collective-permute-start.1 = (bf16[2048,128]{1,0:T(8,128)(2,1)S(1)}, bf16[2048,128]{1,0:T(8,128)(2,1)S(1)}, u32[]{:S(2)}, u32[]{:S(2)}) collective-permute-start(bf16[2048,128]{1,0:T(8,128)(2,1)S(1)} %get-tuple-element.12), channel_id=1, source_target_pairs={{4,0},{8,4},{12,8},{16,12},{20,16},{24,20},{28,24},{5,1},{9,5},{13... | collective-permute-start | bytes 1572872 | tf_op jit(solution)/shard_map/ppermute | solution.py:16
  19.8 5.6 %collective-permute-start.5 = (bf16[3,27,16,128]{3,2,1,0:T(8,128)(2,1)S(1)}, bf16[3,27,16,128]{3,2,1,0:T(8,128)(2,1)S(1)}, u32[]{:S(2)}, u32[]{:S(2)}) collective-permute-start(bf16[3,27,16,128]{3,2,1,0:T(8,128)(2,1)S(1)} %pad_maximum_fusion.got_ref), channel_id=1, source_target_pairs={{0,4},{4,0},{8,12},{12,8},{16,20},{20,16},{24,28},{28,24},{1,5},{5... | collective-permute-start | bytes 995336 | tf_op jit(solution)/shard_map/ppermute | solution.py:479
  31.2 1.2 copy-start.6
  32.4 1.2 copy-start.7
  33.7 136.9 %copy-start.2 = (s32[12288]{0:T(1024)S(1)}, s32[12288]{0:T(1024)}, u32[]{:S(2)}) copy-start(s32[12288]{0:T(1024)} %send_ref.1) | copy-start | bytes 147460
  33.7 136.9 %copy-start.3 = (s32[8192]{0:T(1024)S(1)}, s32[8192]{0:T(1024)}, u32[]{:S(2)}) copy-start(s32[8192]{0:T(1024)} %recv_ref.1) | copy-start | bytes 98308
